TPU v7x, 512 devices: a whole 4x8x8 slice. The times are simulated.
512 devices in a mesh: row: 32 (over x_hi, y, core), col: 16 (over x_lo, z).
Axes of the slice: x: 4 (x_hi: 2, x_lo: 2; x = x_hi * 2 + x_lo), y: 8, z: 8, core: 2. Of those that a mesh axis runs over, the one named last changes fastest.
Arguments:
- click_tiles: bfloat16 [4096, 512, 512], P(('row', 'col')), may hold values from 0 to 20
- tile_coords: int32 [4096, 2], P(('row', 'col')), may hold values from 0 to 7, as said below
- tile_count: int32 [512], P(('row', 'col')), may hold values from 1 to 8, as said below
- prior_labels: float32 [64, 65536], P(None, ('row', 'col')), may hold values from 0.01 to 10
- seed_ids: int32 [16384], P(('row', 'col')), may hold values from 0 to 65535, as said below
- seed_class: int32 [16384], P(('row', 'col')), may hold values from 0 to 63
Outputs:
- query_labels: float32 [64, 65536], P(None, ('row', 'col'))
- url_labels: float32 [64, 65536], P(None, ('col', 'row'))
Inputs may be any that keep to these rules, and one draw needn't show every extreme that they name: `tile_coords`: within each device's 8 slots the (local query block, local URL block) pairs are distinct, first column below 4, second below 8. `tile_count`: some device has all 8 slots live. `seed_ids`: seeds d * 32 to (d + 1) * 32 - 1 name queries d * 128 to (d + 1) * 128 - 1.
All inputs are finite; a program needn't handle non-finite values.
Results may differ from a plain program's by a relative error of at most 0.00097.
Values may be sent and summed in bfloat16 or wider, within the bound.
No kernel may reach another device: no remote copies, remote signals or barrier semaphores. Data moves between devices by JAX's collectives and lax.ppermute only.
A program may use at most 64 MiB of HBM per device.

v0:
```python
import jax
import jax.numpy as jnp
from jax import lax
from jax.sharding import PartitionSpec as P

BC = 8
ITERS = 2


blend_rate = 0.25
seed_weight = 8.0


def shards(click_tiles, tile_coords, tile_count, prior_labels, seed_ids, seed_class):
    col_count = lax.axis_size("col")
    row_count = lax.axis_size("row")
    slots, tile_size = (click_tiles.shape[0], click_tiles.shape[1])
    classes, query_local = prior_labels.shape
    query_slab = query_local * col_count
    query_blocks = query_slab // tile_size
    url_slab = BC * tile_size
    url_local = url_slab // row_count
    highest = lax.Precision.HIGHEST
    active = (jnp.arange(slots) < tile_count[0]).astype(jnp.float32)
    row_onehot = (tile_coords[:, 0:1] == jnp.arange(query_blocks)[None, :]).astype(
        jnp.float32
    ) * active[:, None]
    col_onehot = (tile_coords[:, 1:2] == jnp.arange(BC)[None, :]).astype(jnp.float32) * active[
        :, None
    ]
    ones_side = jnp.ones((tile_size,), jnp.bfloat16)
    row_sums = jnp.einsum("kqu,u->kq", click_tiles, ones_side, preferred_element_type=jnp.float32)
    col_sums = jnp.einsum("kqu,q->ku", click_tiles, ones_side, preferred_element_type=jnp.float32)
    query_part = jnp.einsum("kb,kq->bq", row_onehot, row_sums, precision=highest).reshape(
        query_slab
    )
    url_part = jnp.einsum("kb,ku->bu", col_onehot, col_sums, precision=highest).reshape(url_slab)
    query_deg = lax.psum_scatter(query_part, "col", scatter_dimension=0, tiled=True)
    url_deg = lax.psum_scatter(url_part, "row", scatter_dimension=0, tiled=True)
    offset = (lax.axis_index("row") * col_count + lax.axis_index("col")) * query_local
    local_ids = seed_ids - offset
    class_onehot = (seed_class[:, None] == jnp.arange(classes)[None, :]).astype(jnp.float32)
    place_onehot = (local_ids[:, None] == jnp.arange(query_local)[None, :]).astype(jnp.float32)
    seed_map = jnp.dot(class_onehot.T, place_onehot, precision=highest)
    labels = prior_labels
    url_labels = jnp.zeros((classes, url_local), jnp.float32)
    for iteration in range(ITERS):
        query_rounded = labels.astype(jnp.bfloat16)
        gathered = lax.all_gather(query_rounded, "col", axis=1, tiled=True)
        query_grid = gathered.reshape(classes, query_blocks, tile_size)
        picked = jnp.take(query_grid, tile_coords[:, 0], axis=1)
        products = jnp.einsum(
            "ckq,kqu->kcu", picked, click_tiles, preferred_element_type=jnp.float32
        )
        url_terms = jnp.einsum("kb,kcu->cbu", col_onehot, products, precision=highest).reshape(
            classes, url_slab
        )
        url_share = lax.psum_scatter(url_terms, "row", scatter_dimension=1, tiled=True)
        url_labels = url_share / (url_deg + 1.0)
        url_rounded = url_labels.astype(jnp.bfloat16)
        url_rounded_slab = lax.all_gather(url_rounded, "row", axis=1, tiled=True)
        url_grid = url_rounded_slab.reshape(classes, BC, tile_size)
        url_picked = jnp.take(url_grid, tile_coords[:, 1], axis=1)
        back = jnp.einsum(
            "cku,kqu->kcq", url_picked, click_tiles, preferred_element_type=jnp.float32
        )
        query_terms = jnp.einsum("kb,kcq->cbq", row_onehot, back, precision=highest).reshape(
            classes, query_slab
        )
        query_share = lax.psum_scatter(query_terms, "col", scatter_dimension=1, tiled=True)
        spread = query_share / (query_deg + 1.0)
        labels = (1.0 - blend_rate) * spread + blend_rate * seed_weight * seed_map
    return (labels, url_labels)


def solution(mesh):
    placed = (
        P(("row", "col"), None, None),
        P(("row", "col"), None),
        P(("row", "col")),
        P(None, ("row", "col")),
        P(("row", "col")),
        P(("row", "col")),
    )
    return jax.shard_map(
        shards,
        mesh=mesh,
        in_specs=placed,
        out_specs=(P(None, ("row", "col")), P(None, ("col", "row"))),
        check_vma=False,
    )
```

profile of v0, /device:TPU:12, one launch (start us, length us, event | category | flops | bytes accessed | tf_op | source)
XLA Modules:
  0.0 588.3 jit_solution(448027260249757292)
XLA Ops:
  7.2 0.0 reduce-scatter.5.cloned.1.call-start
  7.2 0.8 slice_bitcast_fusion.1
  8.0 0.8 compare_and_fusion
  9.4 0.8 convert_element_type.23
  10.2 40.6 %all_gather.12 = bf16[64,2048]{1,0:T(8,128)(2,1)S(1)} all-gather(bf16[64,128]{1,0:T(8,128)(2,1)S(1)} %convert_element_type.23), channel_id=1, replica_groups=mesh['row'=32,'col'=16] {'col'}, dimensions={1}, use_global_device_ids=true | all-gather | bytes 278528 | tf_op jit(solution)/shard_map/all_gather | solution.py:49
  50.7 0.6 gather_fusion
  51.3 3.1 fusion.14
  54.4 1.7 fusion.6
  56.1 1.6 copy.31
  57.7 0.0 reduce-scatter.5.cloned.1.call-update
  57.7 0.0 reduce-scatter.7.cloned.1.call-start
  57.8 2.8 fusion.47
  60.6 0.1 convolution_bitcast_fusion
  60.8 1.3 dynamic-slice
  62.7 123.3 %all-reduce = f32[4096]{0:T(1024)S(1)} all-reduce(f32[4096]{0:T(1024)S(1)} %bitcast.96), channel_id=3, replica_groups=mesh['row'=32,'col'=16] {'row'}, use_global_device_ids=true, to_apply=%region_1.3.clone | all-reduce | flops 4096 | bytes 32768
  186.0 0.1 dynamic-slice_add_fusion.1
  186.1 0.0 reduce-scatter.5.cloned.1.call-done
  186.1 0.8 divide_convert_fusion
  186.9 43.6 %all_gather.13 = bf16[64,4096]{1,0:T(8,128)(2,1)S(1)} all-gather(bf16[64,128]{1,0:T(8,128)(2,1)S(1)} %divide_convert_fusion), channel_id=1, replica_groups=mesh['row'=32,'col'=16] {'row'}, dimensions={1}, use_global_device_ids=true | all-gather | bytes 540672 | tf_op jit(solution)/shard_map/all_gather | solution.py:61
  230.5 0.6 gather_fusion.1
  231.1 3.6 fusion.12
  234.7 0.0 copy-start
  234.7 0.0 copy-start.1
  234.7 1.6 fusion.4
  236.3 0.9 copy.33
  237.3 0.0 reduce-scatter.7.cloned.1.call-update
  237.3 0.0 reduce-scatter.9.cloned.1.call-start
  237.3 1.3 dynamic-slice.2
  239.3 3.4 fusion.45
  242.6 0.2 convolution_bitcast_fusion.1
  242.8 31.2 %all-reduce.1 = f32[2048]{0:T(1024)S(1)} all-reduce(f32[2048]{0:T(1024)S(1)} %bitcast.97), channel_id=5, replica_groups=mesh['row'=32,'col'=16] {'col'}, use_global_device_ids=true, to_apply=%region_3.0.clone | all-reduce | flops 2048 | bytes 16384
  274.0 0.1 dynamic-slice_add_fusion
  274.0 0.0 copy-done
  274.0 28.7 %reduce-scatter.7.cloned.1.call-done = f32[64,128]{1,0:T(8,128)} async-done(((f32[64,2048]{1,0:T(8,128)}), f32[64,128]{1,0:T(8,128)}) %reduce-scatter.7.cloned.1.call-update) | async-done | bytes 32784 | tf_op jit(solution)/shard_map/reduce_scatter | solution.py:70
  302.8 0.0 copy-done.1
  302.8 1.0 add_convert_fusion
  303.8 32.3 %all_gather.14 = bf16[64,2048]{1,0:T(8,128)(2,1)S(1)} all-gather(bf16[64,128]{1,0:T(8,128)(2,1)S(1)} %get-tuple-element.14), channel_id=1, replica_groups=mesh['row'=32,'col'=16] {'col'}, dimensions={1}, use_global_device_ids=true | all-gather | bytes 278528 | tf_op jit(solution)/shard_map/all_gather | solution.py:49
  336.2 0.6 gather_fusion.2
  336.7 3.1 fusion.10
  339.8 1.7 fusion.2
  341.5 1.6 copy.35
  343.1 0.0 reduce-scatter.9.cloned.1.call-update
  343.1 0.0 reduce-scatter.11.cloned.1.call-start
  343.2 117.7 %reduce-scatter.9.cloned.1.call-done = f32[64,128]{1,0:T(8,128)} async-done(((f32[64,4096]{1,0:T(8,128)}), f32[64,128]{1,0:T(8,128)}) %reduce-scatter.9.cloned.1.call-update) | async-done | bytes 32784 | tf_op jit(solution)/shard_map/reduce_scatter | solution.py:58
  460.9 1.4 fusion.70
  462.3 38.9 %all_gather.15 = bf16[64,4096]{1,0:T(8,128)(2,1)S(1)} all-gather(bf16[64,128]{1,0:T(8,128)(2,1)S(1)} %get-tuple-element.4), channel_id=1, replica_groups=mesh['row'=32,'col'=16] {'row'}, dimensions={1}, use_global_device_ids=true | all-gather | bytes 540672 | tf_op jit(solution)/shard_map/all_gather | solution.py:61
  501.2 0.6 gather_fusion.3
  501.8 3.6 fusion.8
  505.4 1.6 fusion
  507.0 0.9 copy.36
  508.0 0.0 reduce-scatter.11.cloned.1.call-update
  508.0 72.4 %reduce-scatter.11.cloned.1.call-done = f32[64,128]{1,0:T(8,128)} async-done(((f32[64,2048]{1,0:T(8,128)}), f32[64,128]{1,0:T(8,128)}) %reduce-scatter.11.cloned.1.call-update) | async-done | bytes 32784 | tf_op jit(solution)/shard_map/reduce_scatter | solution.py:70
  580.4 1.4 multiply_add_fusion
  (10 shorter events, 0.2 us)
Async XLA Ops:
  7.2 178.9 %reduce-scatter.5.cloned.1.call-start = ((), (), s32[]{:S(2)}) async-start(), calls=%async_computation.4 | async-start | bytes 1081344 | tf_op jit(solution)/shard_map/reduce_scatter | solution.py:58
  57.7 245.1 %reduce-scatter.7.cloned.1.call-start = ((), (), s32[]{:S(2)}) async-start(), calls=%async_computation.5 | async-start | bytes 557056 | tf_op jit(solution)/shard_map/reduce_scatter | solution.py:70
  234.7 39.3 %copy-start = (s32[32]{0:T(128)S(1)}, s32[32]{0:T(128)}, u32[]{:S(2)}) copy-start(s32[32]{0:T(128)} %param.14) | copy-start | bytes 388
  234.7 68.1 %copy-start.1 = (s32[32]{0:T(128)S(1)}, s32[32]{0:T(128)}, u32[]{:S(2)}) copy-start(s32[32]{0:T(128)} %param.15) | copy-start | bytes 388
  237.3 223.6 %reduce-scatter.9.cloned.1.call-start = ((), (), s32[]{:S(2)}) async-start(), calls=%async_computation.6 | async-start | bytes 1081344 | tf_op jit(solution)/shard_map/reduce_scatter | solution.py:58
  343.1 237.3 %reduce-scatter.11.cloned.1.call-start = ((), (), s32[]{:S(2)}) async-start(), calls=%async_computation.7 | async-start | bytes 557056 | tf_op jit(solution)/shard_map/reduce_scatter | solution.py:70
Sparse Core Ops, SparseCore 0:
  57.8 117.7 reduce-scatter.4
  237.4 65.3 reduce-scatter.6
  343.2 117.6 reduce-scatter.8
  508.1 72.2 reduce-scatter.10
where the time goes:
time: 589 us; the launch traced here: 588 us
  blocking collectives  310 us (53%)
  waiting for transfers between devices  219 us (37%)
  matrix products  27.3 us (5%)
  between operations  15.9 us (3%)
  local copies, waits for them, and re-layouts  10.8 us (2%)
    unnamed x2, blocking collectives  154 us
    reduce_scatter x2, waiting for transfers between devices, shards(): lax.psum_scatter(url_terms, 'row', scatter_dimension=1, tiled=True)  118 us
    reduce_scatter x2, waiting for transfers between devices, shards(): lax.psum_scatter(query_terms, 'col', scatter_dimension=1, tiled=True)  101 us
    all_gather x2, blocking collectives, shards(): url_rounded_slab = lax.all_gather(url_rounded, 'row', axis=1, tiled=True)  82.5 us
    all_gather x2, blocking collectives, shards(): gathered = lax.all_gather(query_rounded, 'col', axis=1, tiled=True)  72.9 us
  transfers between devices with their start and end apart: 4, of which 3 were waited for; matrix products, arithmetic and copies ran while one was open for 2% of the time, Pallas kernels for 0%

commit v1 on v0

v1 whole, which is shorter than its diff:
```python
import jax
import jax.numpy as jnp
from jax import lax
from jax.experimental import pallas as pl
from jax.experimental.pallas import tpu as pltpu
from jax.sharding import Mesh, PartitionSpec as P

BR = 4
BC = 8
ITERS = 2
LANES = 128
EXTRA = 16
SCALE = 512.0

blend_rate = 0.25
seed_weight = 8.0

CHIPS = ("xh", "y")
COL = ("xl", "z")


def url_kernel(slots, meta, labels, tiles, own, other):
    own[...] = jnp.zeros_like(own)
    other[...] = jnp.zeros_like(other)
    core = meta[2 * slots + 1]
    rows = own.shape[1]
    classes = labels.shape[1]
    for k in range(slots):

        @pl.when(k < meta[2 * slots])
        def _():
            a = meta[2 * k]
            b = meta[2 * k + 1]
            left = jnp.concatenate([labels[4 * a + i] for i in range(4)], axis=1)
            if rows > classes:
                left = jnp.concatenate([left, jnp.ones((rows - classes, left.shape[1]), left.dtype)], axis=0)
            for out, parity in ((other, 1 - core), (own, core)):
                near = pl.ds(pl.multiple_of(parity * LANES, LANES), LANES)
                far = pl.ds(pl.multiple_of((parity + 2) * LANES, LANES), LANES)
                right = jnp.concatenate([tiles[k, :, near], tiles[k, :, far]], axis=1)
                term = jnp.dot(left, right, preferred_element_type=jnp.float32)
                out[2 * b] += term[:, :LANES]
                out[2 * b + 1] += term[:, LANES:]


def query_kernel(slots, meta, own, other, tiles, sums):
    sums[...] = jnp.zeros_like(sums)
    core = meta[2 * slots + 1]
    rows = sums.shape[1]
    classes = own.shape[1]
    for k in range(slots):

        @pl.when(k < meta[2 * slots])
        def _():
            a = meta[2 * k]
            b = meta[2 * k + 1]
            term = None
            for labels, parity in ((own, core), (other, 1 - core)):
                near = pl.ds(pl.multiple_of(parity * LANES, LANES), LANES)
                far = pl.ds(pl.multiple_of((parity + 2) * LANES, LANES), LANES)
                left = jnp.concatenate([labels[2 * b], labels[2 * b + 1]], axis=1)
                if rows > classes:
                    left = jnp.concatenate([left, jnp.ones((rows - classes, left.shape[1]), left.dtype)], axis=0)
                right = jnp.concatenate([tiles[k, :, near], tiles[k, :, far]], axis=1)
                part = lax.dot_general(left, right, (((1,), (1,)), ((), ())), preferred_element_type=jnp.float32)
                term = part if term is None else term + part
            for i in range(4):
                sums[4 * a + i] += term[:, i * LANES : (i + 1) * LANES]


def local_call(kernel, meta, operands, out_shape):
    spec = pl.BlockSpec(memory_space=pltpu.VMEM)
    return pl.pallas_call(
        kernel,
        in_specs=[pl.BlockSpec(memory_space=pltpu.SMEM)] + [spec] * len(operands),
        out_specs=jax.tree.map(lambda _: spec, out_shape),
        out_shape=out_shape,
        compiler_params=pltpu.CompilerParams(vmem_limit_bytes=32 * 1024 * 1024),
        cost_estimate=pl.CostEstimate(flops=8 * 2 * 64 * 512 * 512, bytes_accessed=5 << 20, transcendentals=0),
    )(meta, *operands)


def inverse(degree):
    return jnp.where(degree > 0.0, SCALE / jnp.where(degree > 0.0, degree, 1.0), 0.0)


def degree_rows(degree):
    power = jnp.where(degree > 0.0, jnp.floor(jnp.log2(jnp.maximum(degree, 1e-30))), 0.0)
    part = degree * jnp.exp2(-power)
    high = part.astype(jnp.float16)
    low = (part - high.astype(jnp.float32)).astype(jnp.float16)
    return jnp.concatenate([power.astype(jnp.float16), high, low], axis=1)


def degree_of(rows):
    rows = rows.astype(jnp.float32)
    return (rows[:, 1:2] + rows[:, 2:3]) * jnp.exp2(rows[:, 0:1])


def exchange(pieces, axes):
    return lax.all_to_all(pieces, axes, 0, 0, tiled=True)


def spread(piece, axes):
    count = lax.axis_size(axes)
    return exchange(jnp.broadcast_to(piece[None], (count,) + piece.shape), axes)


def reduce(sums, classes, axes, known):
    if known is None:
        degree = sums[:, classes : classes + 1]
        scale = inverse(degree)
        message = jnp.concatenate([(sums[:, :classes] * scale).astype(jnp.float16), degree_rows(degree)], axis=1)
        arrived = exchange(message, axes)
        weights = degree_of(arrived[:, classes:])
        arrived = arrived[:, :classes]
        total = jnp.sum(weights, axis=0) + 1.0
        known = (scale, weights / SCALE, total)
    else:
        arrived = exchange((sums * known[0]).astype(jnp.float16), axes)
    shares = jnp.sum(arrived.astype(jnp.float32) * known[1], axis=0)
    return shares / known[2], known


def shards(click_tiles, tile_coords, tile_count, prior_labels, seed_ids, seed_class):
    slots, tile_size = (click_tiles.shape[0], click_tiles.shape[1])
    classes, query_local = prior_labels.shape
    col_count = lax.axis_size(COL)
    chip_count = lax.axis_size(CHIPS)
    core = lax.axis_index("core").astype(jnp.int32)
    meta = jnp.concatenate([tile_coords.reshape(-1), tile_count, core[None]])

    offset = lax.axis_index(CHIPS + ("core",) + COL) * query_local
    class_onehot = (seed_class[None, :] == jnp.arange(classes)[:, None]).astype(jnp.bfloat16)
    place_onehot = ((seed_ids - offset)[:, None] == jnp.arange(query_local)[None, :]).astype(jnp.bfloat16)
    seed_map = jnp.dot(class_onehot, place_onehot, preferred_element_type=jnp.float32)
    seeds = blend_rate * seed_weight * seed_map

    labels = prior_labels
    url_known = query_known = None
    for iteration in range(ITERS):
        rows = classes + (EXTRA if iteration == 0 else 0)
        gathered = spread(labels.astype(jnp.bfloat16), COL)
        piece = jax.ShapeDtypeStruct((chip_count, rows, LANES), jnp.float32)
        own, other = local_call(
            lambda *refs: url_kernel(slots, *refs), meta, (gathered, click_tiles), (piece, piece)
        )
        if rows > classes:
            own, other = own[:, : classes + 8], other[:, : classes + 8]
        both = own + lax.ppermute(other, "core", [(0, 1), (1, 0)])
        url_labels, url_known = reduce(both, classes, CHIPS, url_known)
        own = spread(url_labels.astype(jnp.bfloat16), CHIPS)
        other = lax.ppermute(own, "core", [(0, 1), (1, 0)])
        sums = local_call(
            lambda *refs: query_kernel(slots, *refs),
            meta,
            (own, other, click_tiles),
            jax.ShapeDtypeStruct((col_count, rows, LANES), jnp.float32),
        )
        mean, query_known = reduce(sums, classes, COL, query_known)
        labels = (1.0 - blend_rate) * mean + seeds
    return labels, url_labels


def solution(mesh):
    grid = Mesh(mesh.devices.reshape(2, 8, 2, 2, 8), ("xh", "y", "core", "xl", "z"))
    row = ("xh", "y", "core")
    everywhere = row + COL
    placed = (
        P(everywhere, None, None),
        P(everywhere, None),
        P(everywhere),
        P(None, everywhere),
        P(everywhere),
        P(everywhere),
    )
    return jax.shard_map(
        shards,
        mesh=grid,
        in_specs=placed,
        out_specs=(P(None, everywhere), P(None, COL + row)),
        check_vma=False,
    )
```

time: 589 us -> 170 us (0.29)
  the two profiles are of different devices: /device:TPU:12 before, /device:TPU:8 now
where the time goes in v1:
time: 170 us
  blocking collectives  104 us (61%)
  waiting for transfers between devices  26.4 us (16%)
  starting transfers between devices  24.1 us (14%)
  local copies, waits for them, and re-layouts  6.16 us (4%)
  other arithmetic  4.02 us (2%)
  Pallas kernels  3.46 us (2%)
    all_to_all x6, blocking collectives, exchange(): return lax.all_to_all(pieces, axes, 0, 0, tiled=True)  104 us
    all_to_all x2, waiting for transfers between devices, exchange(): return lax.all_to_all(pieces, axes, 0, 0, tiled=True)  19.6 us
    all_to_all x2, starting transfers between devices, exchange(): return lax.all_to_all(pieces, axes, 0, 0, tiled=True)  16.2 us
    unnamed x11, local copies, waits for them, and re-layouts  5.15 us
    ppermute x2, starting transfers between devices, shards(): both = own + lax.ppermute(other, 'core', [(0, 1), (1, 0)])  4.1 us
    ppermute x2, waiting for transfers between devices, shards(): both = own + lax.ppermute(other, 'core', [(0, 1), (1, 0)])  3.85 us
    ppermute x2, starting transfers between devices, shards(): other = lax.ppermute(own, 'core', [(0, 1), (1, 0)])  3.82 us
    pallas_call x4, Pallas kernels, local_call(): pl.pallas_call(kernel, in_specs=[pl.BlockSpec(memory_space=pltpu.SMEM)] +...  3.46 us
  transfers between devices with their start and end apart: 6, of which 6 were waited for; matrix products, arithmetic and copies ran while one was open for 1% of the time, Pallas kernels for 0%

profile of v1, /device:TPU:8, one launch (start us, length us, event | category | flops | bytes accessed | tf_op | source)
XLA Modules:
  0.0 169.6 jit_solution(7725297227616002386)
XLA Ops:
  0.6 0.8 convert_element_type.76
  1.4 0.8 broadcast_in_dim.20
  2.1 11.3 %all-to-all-start = ((bf16[16,64,128]{2,1,0:T(8,128)(2,1)}), bf16[16,64,128]{2,1,0:T(8,128)(2,1)S(1)}, u32[]{:S(2)}, u32[]{:S(2)}) async-start(bf16[16,64,128]{2,1,0:T(8,128)(2,1)} %broadcast_in_dim.20), calls=%async_computation | async-start | bytes 524288 | tf_op jit(solution)/shard_map/all_to_all | solution.py:101
  14.2 0.8 copy.10
  14.9 0.1 reshape.57
  15.0 0.1 pad_add_fusion.refs_0_
  15.1 8.5 %all-to-all-done.refs_1_ = bf16[16,64,128]{2,1,0:T(8,128)(2,1)S(1)} async-done(((bf16[16,64,128]{2,1,0:T(8,128)(2,1)}), bf16[16,64,128]{2,1,0:T(8,128)(2,1)S(1)}, u32[]{:S(2)}, u32[]{:S(2)}) %all-to-all-start) | async-done | bytes 262176 | tf_op jit(solution)/shard_map/all_to_all | solution.py:101
  23.6 0.0 copy-start
  23.6 2.2 %copy-done = bf16[8,512,512]{2,1,0:T(8,128)(2,1)S(1)} copy-done((bf16[8,512,512]{2,1,0:T(8,128)(2,1)S(1)}, bf16[8,512,512]{2,1,0:T(8,128)(2,1)}, u32[]{:S(2)}) %copy-start) | copy-done | bytes 4194328
  25.8 0.9 shard_map.77
  26.7 0.0 copy-start.1
  26.7 2.2 %collective-permute-start = (f32[16,72,128]{2,1,0:T(8,128)S(1)}, f32[16,72,128]{2,1,0:T(8,128)S(1)}, u32[]{:S(2)}, u32[]{:S(2)}) collective-permute-start(f32[16,72,128]{2,1,0:T(8,128)S(1)} %slice.49), channel_id=1, source_target_pairs={{0,16},{16,0},{1,17},{17,1},{2,18},{18,2},{3,19},{19,3},{4,20},{20... | collective-permute-start | bytes 1769480 | tf_op jit(solution)/shard_map/ppermute | solution.py:150
  28.9 2.0 %collective-permute-done = f32[16,72,128]{2,1,0:T(8,128)S(1)} collective-permute-done((f32[16,72,128]{2,1,0:T(8,128)S(1)}, f32[16,72,128]{2,1,0:T(8,128)S(1)}, u32[]{:S(2)}, u32[]{:S(2)}) %collective-permute-start) | collective-permute-done | bytes 589856 | tf_op jit(solution)/shard_map/ppermute | solution.py:150
  30.9 0.1 slice_add_fusion
  31.1 0.1 fusion.1
  31.1 0.1 pad_maximum_fusion
  31.3 23.6 %all_to_all.40 = f16[16,67,128]{2,1,0:T(8,128)(2,1)S(1)} all-to-all(f16[16,67,128]{2,1,0:T(8,128)(2,1)S(1)} %pad_maximum_fusion), channel_id=1, replica_groups=mesh['xh'=2,'y'=8,'core'=2,'xl'=2,'z'=8] {'xh','y'}, dimensions={0} | all-to-all | bytes 548864 | tf_op jit(solution)/shard_map/all_to_all | solution.py:101
  55.0 0.1 multiply_reduce_fusion.3
  55.0 0.0 copy-start.3
  55.1 0.0 copy-start.4
  55.1 15.8 %all_to_all.41.refs_1_ = bf16[16,64,128]{2,1,0:T(8,128)(2,1)S(1)} all-to-all(bf16[16,64,128]{2,1,0:T(8,128)(2,1)S(1)} %broadcast_in_dim.22), channel_id=1, replica_groups=mesh['xh'=2,'y'=8,'core'=2,'xl'=2,'z'=8] {'xh','y'}, dimensions={0} | all-to-all | bytes 524288 | tf_op jit(solution)/shard_map/all_to_all | solution.py:101
  70.9 1.9 %collective-permute-start.1 = (bf16[16,64,128]{2,1,0:T(8,128)(2,1)S(1)}, bf16[16,64,128]{2,1,0:T(8,128)(2,1)S(1)}, u32[]{:S(2)}, u32[]{:S(2)}) collective-permute-start(bf16[16,64,128]{2,1,0:T(8,128)(2,1)S(1)} %all_to_all.41.refs_1_), channel_id=1, source_target_pairs={{0,16},{16,0},{1,17},{17,1},{2,18},{18,2},{3,19},{19,3},{4,20},{20... | collective-permute-start | bytes 786440 | tf_op jit(solution)/shard_map/ppermute | solution.py:153
  72.8 1.5 collective-permute-done.1.refs_2_
  74.3 0.0 copy-done.1
  74.4 0.9 shard_map.78
  75.3 0.1 fusion
  75.4 0.9 pad_maximum_fusion.1
  76.3 4.8 %all-to-all-start.3 = ((f16[16,67,128]{2,1,0:T(8,128)(2,1)}), f16[16,67,128]{2,1,0:T(8,128)(2,1)S(1)}, u32[]{:S(2)}, u32[]{:S(2)}) async-start(f16[16,67,128]{2,1,0:T(8,128)(2,1)} %pad_maximum_fusion.1), calls=%async_computation.3 | async-start | bytes 589824 | tf_op jit(solution)/shard_map/all_to_all | solution.py:101
  81.1 0.0 copy-done.3
  81.1 11.0 %all-to-all-done.3 = f16[16,67,128]{2,1,0:T(8,128)(2,1)S(1)} async-done(((f16[16,67,128]{2,1,0:T(8,128)(2,1)}), f16[16,67,128]{2,1,0:T(8,128)(2,1)S(1)}, u32[]{:S(2)}, u32[]{:S(2)}) %all-to-all-start.3) | async-done | bytes 274464 | tf_op jit(solution)/shard_map/all_to_all | solution.py:101
  92.2 0.1 multiply_reduce_fusion.2
  92.3 0.0 copy-done.4
  92.3 0.2 add_convert_fusion
  92.5 0.1 broadcast_in_dim.44
  92.6 14.2 %all_to_all.42.refs_1_ = bf16[16,64,128]{2,1,0:T(8,128)(2,1)S(1)} all-to-all(bf16[16,64,128]{2,1,0:T(8,128)(2,1)S(1)} %broadcast_in_dim.44), channel_id=1, replica_groups=mesh['xh'=2,'y'=8,'core'=2,'xl'=2,'z'=8] {'xl','z'}, dimensions={0} | all-to-all | bytes 524288 | tf_op jit(solution)/shard_map/all_to_all | solution.py:101
  106.8 0.0 copy-start.2
  106.8 2.2 %copy-done.2 = bf16[8,512,512]{2,1,0:T(8,128)(2,1)S(1)} copy-done((bf16[8,512,512]{2,1,0:T(8,128)(2,1)S(1)}, bf16[8,512,512]{2,1,0:T(8,128)(2,1)}, u32[]{:S(2)}) %copy-start.2) | copy-done | bytes 4194328
  109.0 0.8 shard_map.79
  109.8 1.9 %collective-permute-start.2 = (f32[16,64,128]{2,1,0:T(8,128)S(1)}, f32[16,64,128]{2,1,0:T(8,128)S(1)}, u32[]{:S(2)}, u32[]{:S(2)}) collective-permute-start(f32[16,64,128]{2,1,0:T(8,128)S(1)} %get-tuple-element.9), channel_id=1, source_target_pairs={{0,16},{16,0},{1,17},{17,1},{2,18},{18,2},{3,19},{19,3},{4,20},{20... | collective-permute-start | bytes 1572872 | tf_op jit(solution)/shard_map/ppermute | solution.py:150
  111.8 1.9 %collective-permute-done.2 = f32[16,64,128]{2,1,0:T(8,128)S(1)} collective-permute-done((f32[16,64,128]{2,1,0:T(8,128)S(1)}, f32[16,64,128]{2,1,0:T(8,128)S(1)}, u32[]{:S(2)}, u32[]{:S(2)}) %collective-permute-start.2) | collective-permute-done | bytes 524320 | tf_op jit(solution)/shard_map/ppermute | solution.py:150
  113.6 0.1 multiply_convert_fusion.1
  113.7 18.3 %all_to_all.43 = f16[16,64,128]{2,1,0:T(8,128)(2,1)S(1)} all-to-all(f16[16,64,128]{2,1,0:T(8,128)(2,1)S(1)} %multiply_convert_fusion.1), channel_id=1, replica_groups=mesh['xh'=2,'y'=8,'core'=2,'xl'=2,'z'=8] {'xh','y'}, dimensions={0} | all-to-all | bytes 524288 | tf_op jit(solution)/shard_map/all_to_all | solution.py:101
  132.0 0.1 multiply_reduce_fusion.1
  132.1 0.6 fusion.8
  132.7 15.8 %all_to_all.44.refs_1_ = bf16[16,64,128]{2,1,0:T(8,128)(2,1)S(1)} all-to-all(bf16[16,64,128]{2,1,0:T(8,128)(2,1)S(1)} %broadcast_in_dim.45), channel_id=1, replica_groups=mesh['xh'=2,'y'=8,'core'=2,'xl'=2,'z'=8] {'xh','y'}, dimensions={0} | all-to-all | bytes 524288 | tf_op jit(solution)/shard_map/all_to_all | solution.py:101
  148.5 1.9 %collective-permute-start.3 = (bf16[16,64,128]{2,1,0:T(8,128)(2,1)S(1)}, bf16[16,64,128]{2,1,0:T(8,128)(2,1)S(1)}, u32[]{:S(2)}, u32[]{:S(2)}) collective-permute-start(bf16[16,64,128]{2,1,0:T(8,128)(2,1)S(1)} %all_to_all.44.refs_1_), channel_id=1, source_target_pairs={{0,16},{16,0},{1,17},{17,1},{2,18},{18,2},{3,19},{19,3},{4,20},{20... | collective-permute-start | bytes 786440 | tf_op jit(solution)/shard_map/ppermute | solution.py:153
  150.5 1.5 collective-permute-done.3.refs_2_
  152.0 0.9 shard_map.80
  152.8 0.1 multiply_convert_fusion
  152.9 16.0 %all_to_all.45 = f16[16,64,128]{2,1,0:T(8,128)(2,1)S(1)} all-to-all(f16[16,64,128]{2,1,0:T(8,128)(2,1)S(1)} %multiply_convert_fusion), channel_id=1, replica_groups=mesh['xh'=2,'y'=8,'core'=2,'xl'=2,'z'=8] {'xl','z'}, dimensions={0} | all-to-all | bytes 524288 | tf_op jit(solution)/shard_map/all_to_all | solution.py:101
  168.9 0.1 multiply_reduce_fusion
  169.0 0.6 multiply_add_fusion
  (19 shorter events, 0.4 us)
Async XLA Ops:
  2.1 21.5 %all-to-all-start = ((bf16[16,64,128]{2,1,0:T(8,128)(2,1)}), bf16[16,64,128]{2,1,0:T(8,128)(2,1)S(1)}, u32[]{:S(2)}, u32[]{:S(2)}) async-start(bf16[16,64,128]{2,1,0:T(8,128)(2,1)} %broadcast_in_dim.20), calls=%async_computation | async-start | bytes 524288 | tf_op jit(solution)/shard_map/all_to_all | solution.py:101
  23.6 2.2 %copy-start = (bf16[8,512,512]{2,1,0:T(8,128)(2,1)S(1)}, bf16[8,512,512]{2,1,0:T(8,128)(2,1)}, u32[]{:S(2)}) copy-start(bf16[8,512,512]{2,1,0:T(8,128)(2,1)} %refs_3_.3) | copy-start | bytes 12582916
  26.7 47.7 %copy-start.1 = (bf16[8,512,512]{2,1,0:T(8,128)(2,1)S(1)}, bf16[8,512,512]{2,1,0:T(8,128)(2,1)}, u32[]{:S(2)}) copy-start(bf16[8,512,512]{2,1,0:T(8,128)(2,1)} %refs_3_.3) | copy-start | bytes 12582916
  26.7 4.2 %collective-permute-start = (f32[16,72,128]{2,1,0:T(8,128)S(1)}, f32[16,72,128]{2,1,0:T(8,128)S(1)}, u32[]{:S(2)}, u32[]{:S(2)}) collective-permute-start(f32[16,72,128]{2,1,0:T(8,128)S(1)} %slice.49), channel_id=1, source_target_pairs={{0,16},{16,0},{1,17},{17,1},{2,18},{18,2},{3,19},{19,3},{4,20},{20... | collective-permute-start | bytes 1769480 | tf_op jit(solution)/shard_map/ppermute | solution.py:150
  55.0 26.1 %copy-start.3 = (s32[32]{0:T(128)S(1)}, s32[32]{0:T(128)}, u32[]{:S(2)}) copy-start(s32[32]{0:T(128)} %param.10) | copy-start | bytes 388
  55.1 37.2 %copy-start.4 = (s32[32]{0:T(128)S(1)}, s32[32]{0:T(128)}, u32[]{:S(2)}) copy-start(s32[32]{0:T(128)} %param.11) | copy-start | bytes 388
  70.9 3.4 %collective-permute-start.1 = (bf16[16,64,128]{2,1,0:T(8,128)(2,1)S(1)}, bf16[16,64,128]{2,1,0:T(8,128)(2,1)S(1)}, u32[]{:S(2)}, u32[]{:S(2)}) collective-permute-start(bf16[16,64,128]{2,1,0:T(8,128)(2,1)S(1)} %all_to_all.41.refs_1_), channel_id=1, source_target_pairs={{0,16},{16,0},{1,17},{17,1},{2,18},{18,2},{3,19},{19,3},{4,20},{20... | collective-permute-start | bytes 786440 | tf_op jit(solution)/shard_map/ppermute | solution.py:153
  76.3 15.9 %all-to-all-start.3 = ((f16[16,67,128]{2,1,0:T(8,128)(2,1)}), f16[16,67,128]{2,1,0:T(8,128)(2,1)S(1)}, u32[]{:S(2)}, u32[]{:S(2)}) async-start(f16[16,67,128]{2,1,0:T(8,128)(2,1)} %pad_maximum_fusion.1), calls=%async_computation.3 | async-start | bytes 589824 | tf_op jit(solution)/shard_map/all_to_all | solution.py:101
  106.8 2.2 %copy-start.2 = (bf16[8,512,512]{2,1,0:T(8,128)(2,1)S(1)}, bf16[8,512,512]{2,1,0:T(8,128)(2,1)}, u32[]{:S(2)}) copy-start(bf16[8,512,512]{2,1,0:T(8,128)(2,1)} %refs_3_.3) | copy-start | bytes 12582916
  109.8 3.8 %collective-permute-start.2 = (f32[16,64,128]{2,1,0:T(8,128)S(1)}, f32[16,64,128]{2,1,0:T(8,128)S(1)}, u32[]{:S(2)}, u32[]{:S(2)}) collective-permute-start(f32[16,64,128]{2,1,0:T(8,128)S(1)} %get-tuple-element.9), channel_id=1, source_target_pairs={{0,16},{16,0},{1,17},{17,1},{2,18},{18,2},{3,19},{19,3},{4,20},{20... | collective-permute-start | bytes 1572872 | tf_op jit(solution)/shard_map/ppermute | solution.py:150
  148.5 3.4 %collective-permute-start.3 = (bf16[16,64,128]{2,1,0:T(8,128)(2,1)S(1)}, bf16[16,64,128]{2,1,0:T(8,128)(2,1)S(1)}, u32[]{:S(2)}, u32[]{:S(2)}) collective-permute-start(bf16[16,64,128]{2,1,0:T(8,128)(2,1)S(1)} %all_to_all.44.refs_1_), channel_id=1, source_target_pairs={{0,16},{16,0},{1,17},{17,1},{2,18},{18,2},{3,19},{19,3},{4,20},{20... | collective-permute-start | bytes 786440 | tf_op jit(solution)/shard_map/ppermute | solution.py:153

commit v2 on v1

v2 whole, which is shorter than its diff:
```python
import jax
import jax.numpy as jnp
from jax import lax
from jax.experimental import pallas as pl
from jax.experimental.pallas import tpu as pltpu
from jax.sharding import Mesh, PartitionSpec as P

BR = 4
BC = 8
ITERS = 2
LANES = 128
EXTRA = 16
SCALE = 512.0
VMEM_LIMIT = 16 * 1024 * 1024

blend_rate = 0.25
seed_weight = 8.0

CHIPS = ("xh", "y")
COL = ("xl", "z")


def load_kernel(source, loaded, sem):
    copy = pltpu.make_async_copy(source, loaded, sem)
    copy.start()
    copy.wait()


def widened(labels, rows, live):
    if rows > labels.shape[0]:
        ones = jnp.ones((rows - labels.shape[0], labels.shape[1]), labels.dtype)
        labels = jnp.concatenate([labels, ones], axis=0)
    return labels * live


def live_slot(slots, meta, k):
    return (k < meta[2 * slots]).astype(jnp.float32).astype(jnp.bfloat16)


def url_kernel(slots, meta, labels, tiles, own, other, kept):
    own[...] = jnp.zeros_like(own)
    other[...] = jnp.zeros_like(other)
    first = meta[2 * slots + 1] == 0
    for k in range(slots):
        a = meta[2 * k]
        b = meta[2 * k + 1]
        left = jnp.concatenate([labels[4 * a + i] for i in range(4)], axis=1)
        left = widened(left, own.shape[1], live_slot(slots, meta, k))
        term = jnp.dot(left, tiles[k], preferred_element_type=jnp.float32)
        for i in range(2):
            even = term[:, 2 * i * LANES : (2 * i + 1) * LANES]
            odd = term[:, (2 * i + 1) * LANES : (2 * i + 2) * LANES]
            own[2 * b + i] += jnp.where(first, even, odd)
            other[2 * b + i] += jnp.where(first, odd, even)


def query_kernel(slots, meta, labels, tiles, sums, kept):
    sums[...] = jnp.zeros_like(sums)
    for k in range(slots):
        a = meta[2 * k]
        b = meta[2 * k + 1]
        left = jnp.concatenate([labels[j % 2, 2 * b + j // 2] for j in range(4)], axis=1)
        left = widened(left, sums.shape[1], live_slot(slots, meta, k))
        term = lax.dot_general(left, tiles[k], (((1,), (1,)), ((), ())), preferred_element_type=jnp.float32)
        for i in range(4):
            sums[4 * a + i] += term[:, i * LANES : (i + 1) * LANES]


def local_call(kernel, meta, labels, tiles, shapes):
    slots = tiles.shape[0]
    spec = pl.BlockSpec(memory_space=pltpu.VMEM)
    sums = tuple(jax.ShapeDtypeStruct(shape, jnp.float32) for shape in shapes)
    return pl.pallas_call(
        lambda *refs: kernel(slots, *refs),
        in_specs=[pl.BlockSpec(memory_space=pltpu.SMEM), spec, spec],
        out_specs=(spec,) * (len(sums) + 1),
        out_shape=sums + (pltpu.VMEM(tiles.shape, tiles.dtype),),
        input_output_aliases={2: len(sums)},
        compiler_params=pltpu.CompilerParams(vmem_limit_bytes=VMEM_LIMIT),
        cost_estimate=pl.CostEstimate(flops=2 * 64 * 512 * 512 * 8, bytes_accessed=1 << 20, transcendentals=0),
    )(meta, labels, tiles)


def load(tiles):
    return pl.pallas_call(
        load_kernel,
        in_specs=[pl.BlockSpec(memory_space=pltpu.HBM)],
        out_specs=pl.BlockSpec(memory_space=pltpu.VMEM),
        out_shape=pltpu.VMEM(tiles.shape, tiles.dtype),
        scratch_shapes=[pltpu.SemaphoreType.DMA],
        compiler_params=pltpu.CompilerParams(vmem_limit_bytes=VMEM_LIMIT),
        cost_estimate=pl.CostEstimate(flops=0, bytes_accessed=4 << 20, transcendentals=0),
    )(tiles)


def inverse(degree):
    return jnp.where(degree > 0.0, SCALE / jnp.where(degree > 0.0, degree, 1.0), 0.0)


def degree_rows(degree):
    power = jnp.where(degree > 0.0, jnp.floor(jnp.log2(jnp.maximum(degree, 1e-30))), 0.0)
    part = degree * jnp.exp2(-power)
    high = part.astype(jnp.float16)
    low = (part - high.astype(jnp.float32)).astype(jnp.float16)
    return jnp.concatenate([power.astype(jnp.float16), high, low], axis=1)


def degree_of(rows):
    rows = rows.astype(jnp.float32)
    return (rows[:, 1:2] + rows[:, 2:3]) * jnp.exp2(rows[:, 0:1])


def exchange(pieces, axes):
    return lax.all_to_all(pieces, axes, 0, 0, tiled=True)


def spread(piece, axes):
    count = lax.axis_size(axes)
    return exchange(jnp.broadcast_to(piece[None], (count,) + piece.shape).astype(jnp.bfloat16), axes)


def partner(piece, first):
    both = lax.all_gather(piece, "core")
    return jnp.where(first, both[1], both[0])


def joined(own, other, classes, first, known):
    if known is None:
        degree = other[:, classes : classes + 1]
        scale = inverse(degree)
        rest = degree_rows(degree)
        rest = jnp.pad(rest, ((0, 0), (0, EXTRA - rest.shape[1]), (0, 0)))
        arrived = partner(jnp.concatenate([(other[:, :classes] * scale).astype(jnp.float16), rest], axis=1), first)
        degree = degree_of(arrived[:, classes:])
        weights = degree / SCALE
        shares = arrived[:, :classes].astype(jnp.float32) * weights
        come = jnp.concatenate([shares, degree], axis=1)
        return own[:, : classes + 1] + come, (scale, weights)
    arrived = partner((other * known[0]).astype(jnp.float16), first)
    return own + arrived.astype(jnp.float32) * known[1], known


def reduce(sums, classes, axes, known):
    if known is None:
        degree = sums[:, classes : classes + 1]
        scale = inverse(degree)
        message = jnp.concatenate([(sums[:, :classes] * scale).astype(jnp.float16), degree_rows(degree)], axis=1)
        arrived = exchange(message, axes)
        weights = degree_of(arrived[:, classes:])
        arrived = arrived[:, :classes]
        total = jnp.sum(weights, axis=0) + 1.0
        known = (scale, weights / SCALE, total)
    else:
        arrived = exchange((sums * known[0]).astype(jnp.float16), axes)
    shares = jnp.sum(arrived.astype(jnp.float32) * known[1], axis=0)
    return shares / known[2], known


def shards(click_tiles, tile_coords, tile_count, prior_labels, seed_ids, seed_class):
    slots, tile_size = (click_tiles.shape[0], click_tiles.shape[1])
    classes, query_local = prior_labels.shape
    col_count = lax.axis_size(COL)
    chip_count = lax.axis_size(CHIPS)
    core = lax.axis_index("core").astype(jnp.int32)
    meta = jnp.concatenate([tile_coords.reshape(-1), tile_count, core[None]])

    offset = lax.axis_index(CHIPS + ("core",) + COL) * query_local
    class_onehot = (seed_class[None, :] == jnp.arange(classes)[:, None]).astype(jnp.bfloat16)
    place_onehot = ((seed_ids - offset)[:, None] == jnp.arange(query_local)[None, :]).astype(jnp.bfloat16)
    seed_map = jnp.dot(class_onehot, place_onehot, preferred_element_type=jnp.float32)
    seeds = blend_rate * seed_weight * seed_map

    gathered = spread(prior_labels, COL)
    tiles = load(click_tiles)
    gathered, tiles, meta, seeds = lax.optimization_barrier((gathered, tiles, meta, seeds))
    core_known = url_known = query_known = None
    for iteration in range(ITERS):
        rows = classes + (EXTRA if iteration == 0 else 0)
        if iteration > 0:
            gathered = spread(labels.astype(jnp.bfloat16), COL)
        shape = (chip_count, rows, LANES)
        own, other, tiles = local_call(url_kernel, meta, gathered, tiles, (shape, shape))
        both, core_known = joined(own, other, classes, core == 0, core_known)
        url_labels, url_known = reduce(both, classes, CHIPS, url_known)
        both = lax.all_gather(spread(url_labels.astype(jnp.bfloat16), CHIPS), "core")
        sums, tiles = local_call(query_kernel, meta, both, tiles, ((col_count, rows, LANES),))
        mean, query_known = reduce(sums, classes, COL, query_known)
        labels = (1.0 - blend_rate) * mean + seeds
    return labels, url_labels


def solution(mesh):
    grid = Mesh(mesh.devices.reshape(2, 8, 2, 2, 8), ("xh", "y", "core", "xl", "z"))
    row = ("xh", "y", "core")
    everywhere = row + COL
    placed = (
        P(everywhere, None, None),
        P(everywhere, None),
        P(everywhere),
        P(None, everywhere),
        P(everywhere),
        P(everywhere),
    )
    return jax.shard_map(
        shards,
        mesh=grid,
        in_specs=placed,
        out_specs=(P(None, everywhere), P(None, COL + row)),
        check_vma=False,
    )
```

time: 170 us -> 159 us (0.935)
  waiting for transfers between devices: 26.4 us -> 3.91 us
  blocking collectives: 104 us -> 123 us
  starting transfers between devices: 24.1 us -> 11.3 us
  Pallas kernels: 3.46 us -> 7.02 us
  local copies, waits for them, and re-layouts: 6.16 us -> 8.04 us
    all_to_all x2 -> x1, waiting for transfers between devices: 19.6 us -> 3.91 us  [exchange(): return lax.all_to_all(pieces, axes, 0, 0, tiled=True)]
    all_to_all x6 -> x7, blocking collectives: 104 us -> 114 us  [exchange(): return lax.all_to_all(pieces, axes, 0, 0, tiled=True)]
    all_gather x0 -> x4, blocking collectives: none -> 8.79 us  [the longest x2 4.46 us: partner(): both = lax.all_gather(piece, 'core')]
    ppermute x4 -> x0, starting transfers between devices: 7.92 us -> none  [the longest x2 4.1 us: shards(): both = own + lax.ppermute(other, 'core', [(0, 1), (1, 0)])]
    ppermute x4 -> x0, waiting for transfers between devices: 6.85 us -> none  [the longest x2 3.85 us: shards(): both = own + lax.ppermute(other, 'core', [(0, 1), (1, 0)])]
    all_to_all x2 -> x1, starting transfers between devices: 16.2 us -> 11.3 us  [exchange(): return lax.all_to_all(pieces, axes, 0, 0, tiled=True)]
    pallas_call x4 -> x5, Pallas kernels: 3.46 us -> 7.02 us  [the longest x4 6.73 us: local_call(): pl.pallas_call(lambda *refs: kernel(slots, *refs), in_specs=[pl.BlockSpec...]
    unnamed x11, local copies, waits for them, and re-layouts: 5.15 us -> 7.08 us
  transfers between devices with their start and end apart: 6 -> 1, of which waited for: 6 -> 1; matrix products, arithmetic and copies ran while one was open for 1% -> 1% of each run, Pallas kernels for 0% -> 0%
where the time goes in v2:
time: 159 us
  blocking collectives  123 us (77%)
  starting transfers between devices  11.3 us (7%)
  local copies, waits for them, and re-layouts  8.04 us (5%)
  Pallas kernels  7.02 us (4%)
  other arithmetic  3.94 us (2%)
  waiting for transfers between devices  3.91 us (2%)
    all_to_all x7, blocking collectives, exchange(): return lax.all_to_all(pieces, axes, 0, 0, tiled=True)  114 us
    all_to_all x1, starting transfers between devices, exchange(): return lax.all_to_all(pieces, axes, 0, 0, tiled=True)  11.3 us
    unnamed x11, local copies, waits for them, and re-layouts  7.08 us
    pallas_call x4, Pallas kernels, local_call(): pl.pallas_call(lambda *refs: kernel(slots, *refs), in_specs=[pl.BlockSpec...  6.73 us
    all_gather x2, blocking collectives, partner(): both = lax.all_gather(piece, 'core')  4.46 us
    all_gather x2, blocking collectives, shards(): lax.all_gather(spread(url_labels.astype(jnp.bfloat16), CHIPS), 'core')  4.34 us
    all_to_all x1, waiting for transfers between devices, exchange(): return lax.all_to_all(pieces, axes, 0, 0, tiled=True)  3.91 us
  transfers between devices with their start and end apart: 1, of which 1 were waited for; matrix products, arithmetic and copies ran while one was open for 1% of the time, Pallas kernels for 0%

profile of v2, /device:TPU:8, one launch (start us, length us, event | category | flops | bytes accessed | tf_op | source)
XLA Modules:
  0.0 158.8 jit_solution(5282194124347700445)
XLA Ops:
  0.6 0.8 convert_element_type.109
  1.4 0.7 broadcast_in_dim.22
  2.1 11.3 %all-to-all-start = ((bf16[16,64,128]{2,1,0:T(8,128)(2,1)}), bf16[16,64,128]{2,1,0:T(8,128)(2,1)S(1)}, u32[]{:S(2)}, u32[]{:S(2)}) async-start(bf16[16,64,128]{2,1,0:T(8,128)(2,1)} %broadcast_in_dim.22), calls=%async_computation | async-start | bytes 524288 | tf_op jit(solution)/shard_map/all_to_all | solution.py:114
  14.2 0.8 copy.15
  14.9 0.1 reshape.63
  15.0 0.1 pad_add_fusion.refs_0_
  15.1 0.0 copy-start.2
  15.1 2.2 %copy-done.2 = bf16[8,512,512]{2,1,0:T(8,128)(2,1)S(1)} copy-done((bf16[8,512,512]{2,1,0:T(8,128)(2,1)S(1)}, bf16[8,512,512]{2,1,0:T(8,128)(2,1)}, u32[]{:S(2)}) %copy-start.2) | copy-done | bytes 4194328
  17.3 0.0 copy-start.3
  17.3 0.0 copy-start.4
  17.3 0.3 shard_map.77.refs_2_
  17.6 0.0 copy-start
  17.6 1.9 %copy-done = bf16[8,512,512]{2,1,0:T(8,128)(2,1)} copy-done((bf16[8,512,512]{2,1,0:T(8,128)(2,1)}, bf16[8,512,512]{2,1,0:T(8,128)(2,1)S(1)}, u32[]{:S(2)}) %copy-start) | copy-done | bytes 4194328
  19.5 0.0 copy-done.3
  19.5 0.0 copy-done.4
  19.5 0.2 convolution_multiply_fusion
  19.7 3.9 %all-to-all-done.refs_1_ = bf16[16,64,128]{2,1,0:T(8,128)(2,1)S(1)} async-done(((bf16[16,64,128]{2,1,0:T(8,128)(2,1)}), bf16[16,64,128]{2,1,0:T(8,128)(2,1)S(1)}, u32[]{:S(2)}, u32[]{:S(2)}) %all-to-all-start) | async-done | bytes 262176 | tf_op jit(solution)/shard_map/all_to_all | solution.py:114
  23.6 0.0 copy-start.1
  23.6 2.2 %copy-done.1 = bf16[8,512,512]{2,1,0:T(8,128)(2,1)S(1)} copy-done((bf16[8,512,512]{2,1,0:T(8,128)(2,1)S(1)}, bf16[8,512,512]{2,1,0:T(8,128)(2,1)}, u32[]{:S(2)}) %copy-start.1) | copy-done | bytes 4194328
  25.8 1.4 shard_map.78
  27.3 0.1 multiply_convert_fusion.3
  27.4 0.1 fusion.8
  27.4 0.1 pad_maximum_fusion
  27.5 2.3 %all-gather = f16[32,80,128]{2,1,0:T(8,128)(2,1)S(1)} all-gather(f16[16,80,128]{2,1,0:T(8,128)(2,1)S(1)} %pad_maximum_fusion), channel_id=2, replica_groups=mesh['xh'=2,'y'=8,'core'=2,'xl'=2,'z'=8] {'core'}, dimensions={0}, use_global_device_ids=true | all-gather | bytes 983040 | tf_op jit(solution)/shard_map/all_gather | solution.py:123
  29.8 0.1 slice_select_fusion
  30.0 0.1 maximum_add_fusion
  30.2 0.1 fusion
  30.3 0.1 pad_maximum_fusion.1
  30.5 22.1 %all_to_all.40 = f16[16,67,128]{2,1,0:T(8,128)(2,1)S(1)} all-to-all(f16[16,67,128]{2,1,0:T(8,128)(2,1)S(1)} %pad_maximum_fusion.1), channel_id=1, replica_groups=mesh['xh'=2,'y'=8,'core'=2,'xl'=2,'z'=8] {'xh','y'}, dimensions={0} | all-to-all | bytes 548864 | tf_op jit(solution)/shard_map/all_to_all | solution.py:114
  52.6 0.1 multiply_reduce_fusion.3
  52.8 15.8 %all_to_all.41 = bf16[16,64,128]{2,1,0:T(8,128)(2,1)S(1)} all-to-all(bf16[16,64,128]{2,1,0:T(8,128)(2,1)S(1)} %broadcast_in_dim.46), channel_id=1, replica_groups=mesh['xh'=2,'y'=8,'core'=2,'xl'=2,'z'=8] {'xh','y'}, dimensions={0} | all-to-all | bytes 524288 | tf_op jit(solution)/shard_map/all_to_all | solution.py:114
  68.6 2.2 %all-gather.1 = bf16[32,64,128]{2,1,0:T(8,128)(2,1)S(1)} all-gather(bf16[16,64,128]{2,1,0:T(8,128)(2,1)S(1)} %all_to_all.41), channel_id=3, replica_groups=mesh['xh'=2,'y'=8,'core'=2,'xl'=2,'z'=8] {'core'}, dimensions={0}, use_global_device_ids=true | all-gather | bytes 786432 | tf_op jit(solution)/shard_map/all_gather | solution.py:185
  70.7 1.9 %shard_map.79 = (f32[16,80,128]{2,1,0:T(8,128)S(1)}, bf16[8,512,512]{2,1,0:T(8,128)(2,1)S(1)}) custom-call(s32[18]{0:T(128)S(1)} %pad_add_fusion.refs_0_, bf16[2,16,64,128]{3,2,1,0:T(8,128)(2,1)S(1)} %bitcast.10, bf16[8,512,512]{2,1,0:T(8,128)(2,1)S(1)} %get-tuple-element.20.refs_2_), custom_call_target="tpu_custom_call", output_to_operand_aliasing={{1}: (2, {})} | custom-call | flops 268435456 | bytes 1048576 | tf_op jit(solution)/shard_map/pallas_call | solution.py:73
  72.7 0.1 multiply_convert_fusion.2
  72.8 0.1 pad_maximum_fusion.2
  73.0 15.2 %all_to_all.42 = f16[16,67,128]{2,1,0:T(8,128)(2,1)S(1)} all-to-all(f16[16,67,128]{2,1,0:T(8,128)(2,1)S(1)} %pad_maximum_fusion.2), channel_id=1, replica_groups=mesh['xh'=2,'y'=8,'core'=2,'xl'=2,'z'=8] {'xl','z'}, dimensions={0} | all-to-all | bytes 548864 | tf_op jit(solution)/shard_map/all_to_all | solution.py:114
  88.3 0.1 multiply_reduce_fusion.2
  88.4 14.2 %all_to_all.43.refs_1_ = bf16[16,64,128]{2,1,0:T(8,128)(2,1)S(1)} all-to-all(bf16[16,64,128]{2,1,0:T(8,128)(2,1)S(1)} %broadcast_in_dim.47), channel_id=1, replica_groups=mesh['xh'=2,'y'=8,'core'=2,'xl'=2,'z'=8] {'xl','z'}, dimensions={0} | all-to-all | bytes 524288 | tf_op jit(solution)/shard_map/all_to_all | solution.py:114
  102.6 1.4 shard_map.80
  104.1 0.1 multiply_convert_fusion.1
  104.2 2.2 %all-gather.2 = f16[32,64,128]{2,1,0:T(8,128)(2,1)S(1)} all-gather(f16[16,64,128]{2,1,0:T(8,128)(2,1)S(1)} %multiply_convert_fusion.1), channel_id=4, replica_groups=mesh['xh'=2,'y'=8,'core'=2,'xl'=2,'z'=8] {'core'}, dimensions={0}, use_global_device_ids=true | all-gather | bytes 786432 | tf_op jit(solution)/shard_map/all_gather | solution.py:123
  106.3 0.2 fusion.3
  106.5 16.3 %all_to_all.44 = f16[16,64,128]{2,1,0:T(8,128)(2,1)S(1)} all-to-all(f16[16,64,128]{2,1,0:T(8,128)(2,1)S(1)} %fusion.3), channel_id=1, replica_groups=mesh['xh'=2,'y'=8,'core'=2,'xl'=2,'z'=8] {'xh','y'}, dimensions={0} | all-to-all | bytes 524288 | tf_op jit(solution)/shard_map/all_to_all | solution.py:114
  122.8 0.1 multiply_reduce_fusion.1
  122.9 0.6 fusion.17
  123.5 15.8 %all_to_all.45 = bf16[16,64,128]{2,1,0:T(8,128)(2,1)S(1)} all-to-all(bf16[16,64,128]{2,1,0:T(8,128)(2,1)S(1)} %broadcast_in_dim.48), channel_id=1, replica_groups=mesh['xh'=2,'y'=8,'core'=2,'xl'=2,'z'=8] {'xh','y'}, dimensions={0} | all-to-all | bytes 524288 | tf_op jit(solution)/shard_map/all_to_all | solution.py:114
  139.3 2.2 %all-gather.3 = bf16[32,64,128]{2,1,0:T(8,128)(2,1)S(1)} all-gather(bf16[16,64,128]{2,1,0:T(8,128)(2,1)S(1)} %all_to_all.45), channel_id=5, replica_groups=mesh['xh'=2,'y'=8,'core'=2,'xl'=2,'z'=8] {'core'}, dimensions={0}, use_global_device_ids=true | all-gather | bytes 786432 | tf_op jit(solution)/shard_map/all_gather | solution.py:185
  141.5 1.9 %shard_map.81 = (f32[16,64,128]{2,1,0:T(8,128)S(1)}, bf16[8,512,512]{2,1,0:T(8,128)(2,1)S(1)}) custom-call(s32[18]{0:T(128)S(1)} %pad_add_fusion.refs_0_, bf16[2,16,64,128]{3,2,1,0:T(8,128)(2,1)S(1)} %bitcast.9, bf16[8,512,512]{2,1,0:T(8,128)(2,1)S(1)} %get-tuple-element.26.refs_2_), custom_call_target="tpu_custom_call", output_to_operand_aliasing={{1}: (2, {})} | custom-call | flops 268435456 | bytes 1048576 | tf_op jit(solution)/shard_map/pallas_call | solution.py:73
  143.4 0.1 multiply_convert_fusion
  143.5 14.6 %all_to_all.46 = f16[16,64,128]{2,1,0:T(8,128)(2,1)S(1)} all-to-all(f16[16,64,128]{2,1,0:T(8,128)(2,1)S(1)} %multiply_convert_fusion), channel_id=1, replica_groups=mesh['xh'=2,'y'=8,'core'=2,'xl'=2,'z'=8] {'xl','z'}, dimensions={0} | all-to-all | bytes 524288 | tf_op jit(solution)/shard_map/all_to_all | solution.py:114
  158.1 0.1 multiply_reduce_fusion
  158.2 0.6 multiply_add_fusion
  (26 shorter events, 0.6 us)
Async XLA Ops:
  2.1 21.5 %all-to-all-start = ((bf16[16,64,128]{2,1,0:T(8,128)(2,1)}), bf16[16,64,128]{2,1,0:T(8,128)(2,1)S(1)}, u32[]{:S(2)}, u32[]{:S(2)}) async-start(bf16[16,64,128]{2,1,0:T(8,128)(2,1)} %broadcast_in_dim.22), calls=%async_computation | async-start | bytes 524288 | tf_op jit(solution)/shard_map/all_to_all | solution.py:114
  15.1 2.2 %copy-start.2 = (bf16[8,512,512]{2,1,0:T(8,128)(2,1)S(1)}, bf16[8,512,512]{2,1,0:T(8,128)(2,1)}, u32[]{:S(2)}) copy-start(bf16[8,512,512]{2,1,0:T(8,128)(2,1)} %source.1) | copy-start | bytes 12582916
  17.3 2.2 %copy-start.3 = (s32[32]{0:T(128)S(1)}, s32[32]{0:T(128)}, u32[]{:S(2)}) copy-start(s32[32]{0:T(128)} %param.10) | copy-start | bytes 388
  17.3 2.2 %copy-start.4 = (s32[32]{0:T(128)S(1)}, s32[32]{0:T(128)}, u32[]{:S(2)}) copy-start(s32[32]{0:T(128)} %param.11) | copy-start | bytes 388
  17.6 1.9 %copy-start = (bf16[8,512,512]{2,1,0:T(8,128)(2,1)}, bf16[8,512,512]{2,1,0:T(8,128)(2,1)S(1)}, u32[]{:S(2)}) copy-start(bf16[8,512,512]{2,1,0:T(8,128)(2,1)S(1)} %shard_map.77.refs_2_) | copy-start | bytes 12582916
  23.6 2.2 %copy-start.1 = (bf16[8,512,512]{2,1,0:T(8,128)(2,1)S(1)}, bf16[8,512,512]{2,1,0:T(8,128)(2,1)}, u32[]{:S(2)}) copy-start(bf16[8,512,512]{2,1,0:T(8,128)(2,1)} %copy-done) | copy-start | bytes 12582916

commit v3 on v2

--- a/solution.py
+++ b/solution.py
@@ -37,16 +37,25 @@
     return (k < meta[2 * slots]).astype(jnp.float32).astype(jnp.bfloat16)
 
 
-def url_kernel(slots, meta, labels, tiles, own, other, kept):
+def fetch(tiles, held, sem):
+    copy = pltpu.make_async_copy(tiles, held, sem)
+    copy.start()
+    return copy
+
+
+def url_kernel(slots, meta, labels, tiles, own, other, *refs):
+    held, sem = refs[-2:]
+    copy = fetch(tiles, held, sem)
     own[...] = jnp.zeros_like(own)
     other[...] = jnp.zeros_like(other)
     first = meta[2 * slots + 1] == 0
+    copy.wait()
     for k in range(slots):
         a = meta[2 * k]
         b = meta[2 * k + 1]
         left = jnp.concatenate([labels[4 * a + i] for i in range(4)], axis=1)
         left = widened(left, own.shape[1], live_slot(slots, meta, k))
-        term = jnp.dot(left, tiles[k], preferred_element_type=jnp.float32)
+        term = jnp.dot(left, held[k], preferred_element_type=jnp.float32)
         for i in range(2):
             even = term[:, 2 * i * LANES : (2 * i + 1) * LANES]
             odd = term[:, (2 * i + 1) * LANES : (2 * i + 2) * LANES]
@@ -54,28 +63,36 @@
             other[2 * b + i] += jnp.where(first, odd, even)
 
 
-def query_kernel(slots, meta, labels, tiles, sums, kept):
+def query_kernel(slots, meta, labels, tiles, sums, *refs):
+    held, sem = refs[-2:]
+    copy = fetch(tiles, held, sem)
     sums[...] = jnp.zeros_like(sums)
+    copy.wait()
     for k in range(slots):
         a = meta[2 * k]
         b = meta[2 * k + 1]
         left = jnp.concatenate([labels[j % 2, 2 * b + j // 2] for j in range(4)], axis=1)
         left = widened(left, sums.shape[1], live_slot(slots, meta, k))
-        term = lax.dot_general(left, tiles[k], (((1,), (1,)), ((), ())), preferred_element_type=jnp.float32)
+        term = lax.dot_general(left, held[k], (((1,), (1,)), ((), ())), preferred_element_type=jnp.float32)
         for i in range(4):
             sums[4 * a + i] += term[:, i * LANES : (i + 1) * LANES]
 
 
-def local_call(kernel, meta, labels, tiles, shapes):
+def local_call(kernel, meta, labels, tiles, shapes, last=False):
     slots = tiles.shape[0]
     spec = pl.BlockSpec(memory_space=pltpu.VMEM)
-    sums = tuple(jax.ShapeDtypeStruct(shape, jnp.float32) for shape in shapes)
+    there = pl.BlockSpec(memory_space=pl.ANY)
+    out_shape = tuple(jax.ShapeDtypeStruct(shape, jnp.float32) for shape in shapes)
+    aliases = {} if last else {2: len(out_shape)}
+    if not last:
+        out_shape += (jax.ShapeDtypeStruct(tiles.shape, tiles.dtype),)
     return pl.pallas_call(
         lambda *refs: kernel(slots, *refs),
-        in_specs=[pl.BlockSpec(memory_space=pltpu.SMEM), spec, spec],
-        out_specs=(spec,) * (len(sums) + 1),
-        out_shape=sums + (pltpu.VMEM(tiles.shape, tiles.dtype),),
-        input_output_aliases={2: len(sums)},
+        in_specs=[pl.BlockSpec(memory_space=pltpu.SMEM), spec, there],
+        out_specs=(spec,) * len(shapes) + (there,) * (len(out_shape) - len(shapes)),
+        out_shape=out_shape,
+        scratch_shapes=[pltpu.VMEM(tiles.shape, tiles.dtype), pltpu.SemaphoreType.DMA],
+        input_output_aliases=aliases,
         compiler_params=pltpu.CompilerParams(vmem_limit_bytes=VMEM_LIMIT),
         cost_estimate=pl.CostEstimate(flops=2 * 64 * 512 * 512 * 8, bytes_accessed=1 << 20, transcendentals=0),
     )(meta, labels, tiles)
@@ -86,7 +103,7 @@
         load_kernel,
         in_specs=[pl.BlockSpec(memory_space=pltpu.HBM)],
         out_specs=pl.BlockSpec(memory_space=pltpu.VMEM),
-        out_shape=pltpu.VMEM(tiles.shape, tiles.dtype),
+        out_shape=jax.ShapeDtypeStruct(tiles.shape, tiles.dtype),
         scratch_shapes=[pltpu.SemaphoreType.DMA],
         compiler_params=pltpu.CompilerParams(vmem_limit_bytes=VMEM_LIMIT),
         cost_estimate=pl.CostEstimate(flops=0, bytes_accessed=4 << 20, transcendentals=0),
@@ -183,7 +200,9 @@
         both, core_known = joined(own, other, classes, core == 0, core_known)
         url_labels, url_known = reduce(both, classes, CHIPS, url_known)
         both = lax.all_gather(spread(url_labels.astype(jnp.bfloat16), CHIPS), "core")
-        sums, tiles = local_call(query_kernel, meta, both, tiles, ((col_count, rows, LANES),))
+        last = iteration == ITERS - 1
+        sums, *rest = local_call(query_kernel, meta, both, tiles, ((col_count, rows, LANES),), last)
+        tiles = rest[0] if rest else tiles
         mean, query_known = reduce(sums, classes, COL, query_known)
         labels = (1.0 - blend_rate) * mean + seeds
     return labels, url_labels

time: 159 us -> 161 us (1.013)
  no operation moved by 1% of the time
where the time goes in v3:
time: 161 us; the launch traced here: 160 us
  blocking collectives  123 us (76%)
  starting transfers between devices  11.3 us (7%)
  Pallas kernels  8.42 us (5%)
  local copies, waits for them, and re-layouts  8.02 us (5%)
  other arithmetic  3.94 us (2%)
  waiting for transfers between devices  3.92 us (2%)
    all_to_all x7, blocking collectives, exchange(): return lax.all_to_all(pieces, axes, 0, 0, tiled=True)  114 us
    all_to_all x1, starting transfers between devices, exchange(): return lax.all_to_all(pieces, axes, 0, 0, tiled=True)  11.3 us
    pallas_call x4, Pallas kernels, local_call(): pl.pallas_call(lambda *refs: kernel(slots, *refs), in_specs=[pl.BlockSpec...  8.13 us
    unnamed x11, local copies, waits for them, and re-layouts  7.07 us
    all_gather x2, blocking collectives, partner(): both = lax.all_gather(piece, 'core')  4.46 us
    all_gather x2, blocking collectives, shards(): lax.all_gather(spread(url_labels.astype(jnp.bfloat16), CHIPS), 'core')  4.34 us
    all_to_all x1, waiting for transfers between devices, exchange(): return lax.all_to_all(pieces, axes, 0, 0, tiled=True)  3.92 us
  transfers between devices with their start and end apart: 1, of which 1 were waited for; matrix products, arithmetic and copies ran while one was open for 1% of the time, Pallas kernels for 0%

profile of v3, /device:TPU:8, one launch (start us, length us, event | category | flops | bytes accessed | tf_op | source)
XLA Modules:
  0.0 160.2 jit_solution(14280092600270721572)
XLA Ops:
  0.6 0.8 convert_element_type.109
  1.4 0.7 broadcast_in_dim.22
  2.1 11.3 %all-to-all-start = ((bf16[16,64,128]{2,1,0:T(8,128)(2,1)}), bf16[16,64,128]{2,1,0:T(8,128)(2,1)S(1)}, u32[]{:S(2)}, u32[]{:S(2)}) async-start(bf16[16,64,128]{2,1,0:T(8,128)(2,1)} %broadcast_in_dim.22), calls=%async_computation | async-start | bytes 524288 | tf_op jit(solution)/shard_map/all_to_all | solution.py:131
  14.1 0.8 copy.14
  14.9 0.1 reshape.63
  15.0 0.1 pad_add_fusion.refs_0_
  15.1 0.0 copy-start.2
  15.1 2.2 %copy-done.2 = bf16[8,512,512]{2,1,0:T(8,128)(2,1)S(1)} copy-done((bf16[8,512,512]{2,1,0:T(8,128)(2,1)S(1)}, bf16[8,512,512]{2,1,0:T(8,128)(2,1)}, u32[]{:S(2)}) %copy-start.2) | copy-done | bytes 4194328
  17.3 0.0 copy-start.3
  17.3 0.0 copy-start.4
  17.3 0.3 shard_map.77.refs_2_
  17.6 0.0 copy-start
  17.6 1.9 %copy-done = bf16[8,512,512]{2,1,0:T(8,128)(2,1)} copy-done((bf16[8,512,512]{2,1,0:T(8,128)(2,1)}, bf16[8,512,512]{2,1,0:T(8,128)(2,1)S(1)}, u32[]{:S(2)}) %copy-start) | copy-done | bytes 4194328
  19.5 0.0 copy-done.3
  19.5 0.0 copy-done.4
  19.5 0.2 convolution_multiply_fusion
  19.7 3.9 %all-to-all-done.refs_1_ = bf16[16,64,128]{2,1,0:T(8,128)(2,1)S(1)} async-done(((bf16[16,64,128]{2,1,0:T(8,128)(2,1)}), bf16[16,64,128]{2,1,0:T(8,128)(2,1)S(1)}, u32[]{:S(2)}, u32[]{:S(2)}) %all-to-all-start) | async-done | bytes 262176 | tf_op jit(solution)/shard_map/all_to_all | solution.py:131
  23.6 0.0 copy-start.1
  23.6 2.2 %copy-done.1 = bf16[8,512,512]{2,1,0:T(8,128)(2,1)S(1)} copy-done((bf16[8,512,512]{2,1,0:T(8,128)(2,1)S(1)}, bf16[8,512,512]{2,1,0:T(8,128)(2,1)}, u32[]{:S(2)}) %copy-start.1) | copy-done | bytes 4194328
  25.8 1.8 %shard_map.78 = (f32[16,80,128]{2,1,0:T(8,128)S(1)}, f32[16,80,128]{2,1,0:T(8,128)S(1)}, bf16[8,512,512]{2,1,0:T(8,128)(2,1)S(1)}) custom-call(s32[18]{0:T(128)S(1)} %pad_add_fusion.refs_0_, bf16[16,64,128]{2,1,0:T(8,128)(2,1)S(1)} %all-to-all-done.refs_1_, bf16[8,512,512]{2,1,0:T(8,128)(2,1)S(1)} %copy-done.1), custom_call_target="tpu_custom_call", output_to_operand_aliasing={{2}: (2, {})} | custom-call | flops 268435456 | bytes 1048576 | tf_op jit(solution)/shard_map/pallas_call | solution.py:89
  27.7 0.1 multiply_convert_fusion.3
  27.8 0.1 fusion.8
  27.8 0.1 pad_maximum_fusion
  27.9 2.3 %all-gather = f16[32,80,128]{2,1,0:T(8,128)(2,1)S(1)} all-gather(f16[16,80,128]{2,1,0:T(8,128)(2,1)S(1)} %pad_maximum_fusion), channel_id=2, replica_groups=mesh['xh'=2,'y'=8,'core'=2,'xl'=2,'z'=8] {'core'}, dimensions={0}, use_global_device_ids=true | all-gather | bytes 983040 | tf_op jit(solution)/shard_map/all_gather | solution.py:140
  30.2 0.1 slice_select_fusion
  30.4 0.1 maximum_add_fusion
  30.6 0.1 fusion
  30.7 0.1 pad_maximum_fusion.1
  30.8 22.1 %all_to_all.40 = f16[16,67,128]{2,1,0:T(8,128)(2,1)S(1)} all-to-all(f16[16,67,128]{2,1,0:T(8,128)(2,1)S(1)} %pad_maximum_fusion.1), channel_id=1, replica_groups=mesh['xh'=2,'y'=8,'core'=2,'xl'=2,'z'=8] {'xh','y'}, dimensions={0} | all-to-all | bytes 548864 | tf_op jit(solution)/shard_map/all_to_all | solution.py:131
  53.0 0.1 multiply_reduce_fusion.3
  53.1 15.8 %all_to_all.41 = bf16[16,64,128]{2,1,0:T(8,128)(2,1)S(1)} all-to-all(bf16[16,64,128]{2,1,0:T(8,128)(2,1)S(1)} %broadcast_in_dim.46), channel_id=1, replica_groups=mesh['xh'=2,'y'=8,'core'=2,'xl'=2,'z'=8] {'xh','y'}, dimensions={0} | all-to-all | bytes 524288 | tf_op jit(solution)/shard_map/all_to_all | solution.py:131
  68.9 2.2 %all-gather.1 = bf16[32,64,128]{2,1,0:T(8,128)(2,1)S(1)} all-gather(bf16[16,64,128]{2,1,0:T(8,128)(2,1)S(1)} %all_to_all.41), channel_id=3, replica_groups=mesh['xh'=2,'y'=8,'core'=2,'xl'=2,'z'=8] {'core'}, dimensions={0}, use_global_device_ids=true | all-gather | bytes 786432 | tf_op jit(solution)/shard_map/all_gather | solution.py:202
  71.1 2.3 %shard_map.79 = (f32[16,80,128]{2,1,0:T(8,128)S(1)}, bf16[8,512,512]{2,1,0:T(8,128)(2,1)S(1)}) custom-call(s32[18]{0:T(128)S(1)} %pad_add_fusion.refs_0_, bf16[2,16,64,128]{3,2,1,0:T(8,128)(2,1)S(1)} %bitcast.9, bf16[8,512,512]{2,1,0:T(8,128)(2,1)S(1)} %get-tuple-element.19.refs_2_), custom_call_target="tpu_custom_call", output_to_operand_aliasing={{1}: (2, {})} | custom-call | flops 268435456 | bytes 1048576 | tf_op jit(solution)/shard_map/pallas_call | solution.py:89
  73.5 0.1 multiply_convert_fusion.2
  73.6 0.1 pad_maximum_fusion.2
  73.7 15.2 %all_to_all.42 = f16[16,67,128]{2,1,0:T(8,128)(2,1)S(1)} all-to-all(f16[16,67,128]{2,1,0:T(8,128)(2,1)S(1)} %pad_maximum_fusion.2), channel_id=1, replica_groups=mesh['xh'=2,'y'=8,'core'=2,'xl'=2,'z'=8] {'xl','z'}, dimensions={0} | all-to-all | bytes 548864 | tf_op jit(solution)/shard_map/all_to_all | solution.py:131
  89.0 0.1 multiply_reduce_fusion.2
  89.1 14.2 %all_to_all.43.refs_1_ = bf16[16,64,128]{2,1,0:T(8,128)(2,1)S(1)} all-to-all(bf16[16,64,128]{2,1,0:T(8,128)(2,1)S(1)} %broadcast_in_dim.47), channel_id=1, replica_groups=mesh['xh'=2,'y'=8,'core'=2,'xl'=2,'z'=8] {'xl','z'}, dimensions={0} | all-to-all | bytes 524288 | tf_op jit(solution)/shard_map/all_to_all | solution.py:131
  103.4 1.8 %shard_map.80 = (f32[16,64,128]{2,1,0:T(8,128)S(1)}, f32[16,64,128]{2,1,0:T(8,128)S(1)}, bf16[8,512,512]{2,1,0:T(8,128)(2,1)S(1)}) custom-call(s32[18]{0:T(128)S(1)} %pad_add_fusion.refs_0_, bf16[16,64,128]{2,1,0:T(8,128)(2,1)S(1)} %all_to_all.43.refs_1_, bf16[8,512,512]{2,1,0:T(8,128)(2,1)S(1)} %get-tuple-element.22.refs_2_), custom_call_target="tpu_custom_call", output_to_operand_aliasing={{2}: (2, {})} | custom-call | flops 268435456 | bytes 1048576 | tf_op jit(solution)/shard_map/pallas_call | solution.py:89
  105.2 0.1 multiply_convert_fusion.1
  105.2 2.2 %all-gather.2 = f16[32,64,128]{2,1,0:T(8,128)(2,1)S(1)} all-gather(f16[16,64,128]{2,1,0:T(8,128)(2,1)S(1)} %multiply_convert_fusion.1), channel_id=4, replica_groups=mesh['xh'=2,'y'=8,'core'=2,'xl'=2,'z'=8] {'core'}, dimensions={0}, use_global_device_ids=true | all-gather | bytes 786432 | tf_op jit(solution)/shard_map/all_gather | solution.py:140
  107.4 0.2 fusion.3
  107.6 16.3 %all_to_all.44 = f16[16,64,128]{2,1,0:T(8,128)(2,1)S(1)} all-to-all(f16[16,64,128]{2,1,0:T(8,128)(2,1)S(1)} %fusion.3), channel_id=1, replica_groups=mesh['xh'=2,'y'=8,'core'=2,'xl'=2,'z'=8] {'xh','y'}, dimensions={0} | all-to-all | bytes 524288 | tf_op jit(solution)/shard_map/all_to_all | solution.py:131
  123.9 0.1 multiply_reduce_fusion.1
  123.9 0.6 fusion.17
  124.6 15.8 %all_to_all.45 = bf16[16,64,128]{2,1,0:T(8,128)(2,1)S(1)} all-to-all(bf16[16,64,128]{2,1,0:T(8,128)(2,1)S(1)} %broadcast_in_dim.48), channel_id=1, replica_groups=mesh['xh'=2,'y'=8,'core'=2,'xl'=2,'z'=8] {'xh','y'}, dimensions={0} | all-to-all | bytes 524288 | tf_op jit(solution)/shard_map/all_to_all | solution.py:131
  140.4 2.2 %all-gather.3 = bf16[32,64,128]{2,1,0:T(8,128)(2,1)S(1)} all-gather(bf16[16,64,128]{2,1,0:T(8,128)(2,1)S(1)} %all_to_all.45), channel_id=5, replica_groups=mesh['xh'=2,'y'=8,'core'=2,'xl'=2,'z'=8] {'core'}, dimensions={0}, use_global_device_ids=true | all-gather | bytes 786432 | tf_op jit(solution)/shard_map/all_gather | solution.py:202
  142.6 2.3 %shard_map.81 = f32[16,64,128]{2,1,0:T(8,128)S(1)} custom-call(s32[18]{0:T(128)S(1)} %pad_add_fusion.refs_0_, bf16[2,16,64,128]{3,2,1,0:T(8,128)(2,1)S(1)} %bitcast.10, bf16[8,512,512]{2,1,0:T(8,128)(2,1)S(1)} %get-tuple-element.25.refs_2_), custom_call_target="tpu_custom_call" | custom-call | flops 268435456 | bytes 1048576 | tf_op jit(solution)/shard_map/pallas_call | solution.py:89
  144.9 0.1 multiply_convert_fusion
  144.9 14.6 %all_to_all.46 = f16[16,64,128]{2,1,0:T(8,128)(2,1)S(1)} all-to-all(f16[16,64,128]{2,1,0:T(8,128)(2,1)S(1)} %multiply_convert_fusion), channel_id=1, replica_groups=mesh['xh'=2,'y'=8,'core'=2,'xl'=2,'z'=8] {'xl','z'}, dimensions={0} | all-to-all | bytes 524288 | tf_op jit(solution)/shard_map/all_to_all | solution.py:131
  159.5 0.1 multiply_reduce_fusion
  159.6 0.6 multiply_add_fusion
  (26 shorter events, 0.6 us)
Async XLA Ops:
  2.1 21.5 %all-to-all-start = ((bf16[16,64,128]{2,1,0:T(8,128)(2,1)}), bf16[16,64,128]{2,1,0:T(8,128)(2,1)S(1)}, u32[]{:S(2)}, u32[]{:S(2)}) async-start(bf16[16,64,128]{2,1,0:T(8,128)(2,1)} %broadcast_in_dim.22), calls=%async_computation | async-start | bytes 524288 | tf_op jit(solution)/shard_map/all_to_all | solution.py:131
  15.1 2.2 %copy-start.2 = (bf16[8,512,512]{2,1,0:T(8,128)(2,1)S(1)}, bf16[8,512,512]{2,1,0:T(8,128)(2,1)}, u32[]{:S(2)}) copy-start(bf16[8,512,512]{2,1,0:T(8,128)(2,1)} %source.1) | copy-start | bytes 12582916
  17.3 2.2 %copy-start.3 = (s32[32]{0:T(128)S(1)}, s32[32]{0:T(128)}, u32[]{:S(2)}) copy-start(s32[32]{0:T(128)} %param.10) | copy-start | bytes 388
  17.3 2.2 %copy-start.4 = (s32[32]{0:T(128)S(1)}, s32[32]{0:T(128)}, u32[]{:S(2)}) copy-start(s32[32]{0:T(128)} %param.11) | copy-start | bytes 388
  17.6 1.9 %copy-start = (bf16[8,512,512]{2,1,0:T(8,128)(2,1)}, bf16[8,512,512]{2,1,0:T(8,128)(2,1)S(1)}, u32[]{:S(2)}) copy-start(bf16[8,512,512]{2,1,0:T(8,128)(2,1)S(1)} %shard_map.77.refs_2_) | copy-start | bytes 12582916
  23.6 2.2 %copy-start.1 = (bf16[8,512,512]{2,1,0:T(8,128)(2,1)S(1)}, bf16[8,512,512]{2,1,0:T(8,128)(2,1)}, u32[]{:S(2)}) copy-start(bf16[8,512,512]{2,1,0:T(8,128)(2,1)} %copy-done) | copy-start | bytes 12582916

commit v4 on v3

--- a/solution.py
+++ b/solution.py
@@ -68,6 +68,18 @@
     copy = fetch(tiles, held, sem)
     sums[...] = jnp.zeros_like(sums)
     copy.wait()
+    query_sums(slots, meta, labels, held, sums)
+
+
+def last_kernel(slots, meta, labels, tiles, scores, sums, result, sem):
+    copy = pltpu.make_async_copy(scores, result, sem)
+    copy.start()
+    sums[...] = jnp.zeros_like(sums)
+    query_sums(slots, meta, labels, tiles, sums)
+    copy.wait()
+
+
+def query_sums(slots, meta, labels, held, sums):
     for k in range(slots):
         a = meta[2 * k]
         b = meta[2 * k + 1]
@@ -78,24 +90,41 @@
             sums[4 * a + i] += term[:, i * LANES : (i + 1) * LANES]
 
 
-def local_call(kernel, meta, labels, tiles, shapes, last=False):
+COST = pl.CostEstimate(flops=2 * 64 * 512 * 512 * 8, bytes_accessed=1 << 20, transcendentals=0)
+
+
+def local_call(kernel, meta, labels, tiles, shapes):
     slots = tiles.shape[0]
     spec = pl.BlockSpec(memory_space=pltpu.VMEM)
     there = pl.BlockSpec(memory_space=pl.ANY)
-    out_shape = tuple(jax.ShapeDtypeStruct(shape, jnp.float32) for shape in shapes)
-    aliases = {} if last else {2: len(out_shape)}
-    if not last:
-        out_shape += (jax.ShapeDtypeStruct(tiles.shape, tiles.dtype),)
+    sums = tuple(jax.ShapeDtypeStruct(shape, jnp.float32) for shape in shapes)
     return pl.pallas_call(
         lambda *refs: kernel(slots, *refs),
         in_specs=[pl.BlockSpec(memory_space=pltpu.SMEM), spec, there],
-        out_specs=(spec,) * len(shapes) + (there,) * (len(out_shape) - len(shapes)),
-        out_shape=out_shape,
+        out_specs=(spec,) * len(sums) + (there,),
+        out_shape=sums + (jax.ShapeDtypeStruct(tiles.shape, tiles.dtype),),
         scratch_shapes=[pltpu.VMEM(tiles.shape, tiles.dtype), pltpu.SemaphoreType.DMA],
-        input_output_aliases=aliases,
+        input_output_aliases={2: len(sums)},
         compiler_params=pltpu.CompilerParams(vmem_limit_bytes=VMEM_LIMIT),
-        cost_estimate=pl.CostEstimate(flops=2 * 64 * 512 * 512 * 8, bytes_accessed=1 << 20, transcendentals=0),
+        cost_estimate=COST,
     )(meta, labels, tiles)
+
+
+def last_call(meta, labels, tiles, scores, shape):
+    slots = tiles.shape[0]
+    spec = pl.BlockSpec(memory_space=pltpu.VMEM)
+    return pl.pallas_call(
+        lambda *refs: last_kernel(slots, *refs),
+        in_specs=[pl.BlockSpec(memory_space=pltpu.SMEM), spec, spec, spec],
+        out_specs=(spec, pl.BlockSpec(memory_space=pl.ANY)),
+        out_shape=(
+            jax.ShapeDtypeStruct(shape, jnp.float32),
+            jax.ShapeDtypeStruct(scores.shape, scores.dtype),
+        ),
+        scratch_shapes=[pltpu.SemaphoreType.DMA],
+        compiler_params=pltpu.CompilerParams(vmem_limit_bytes=VMEM_LIMIT),
+        cost_estimate=COST,
+    )(meta, labels, tiles, scores)
 
 
 def load(tiles):
@@ -200,9 +229,11 @@
         both, core_known = joined(own, other, classes, core == 0, core_known)
         url_labels, url_known = reduce(both, classes, CHIPS, url_known)
         both = lax.all_gather(spread(url_labels.astype(jnp.bfloat16), CHIPS), "core")
-        last = iteration == ITERS - 1
-        sums, *rest = local_call(query_kernel, meta, both, tiles, ((col_count, rows, LANES),), last)
-        tiles = rest[0] if rest else tiles
+        shape = (col_count, rows, LANES)
+        if iteration < ITERS - 1:
+            sums, tiles = local_call(query_kernel, meta, both, tiles, (shape,))
+        else:
+            sums, url_labels = last_call(meta, both, tiles, url_labels, shape)
         mean, query_known = reduce(sums, classes, COL, query_known)
         labels = (1.0 - blend_rate) * mean + seeds
     return labels, url_labels

time: 161 us -> 160 us (level)
    pallas_call x4 -> x3, Pallas kernels: 8.13 us -> 5.86 us  [local_call(): pl.pallas_call(lambda *refs: kernel(slots, *refs), in_specs=[pl.BlockSpec...]
    pallas_call x0 -> x1, Pallas kernels: none -> 1.95 us  [last_call(): pl.pallas_call(lambda *refs: last_kernel(slots, *refs), in_specs=[pl.Bloc...]
where the time goes in v4:
time: 160 us; the launch traced here: 159 us
  blocking collectives  123 us (77%)
  starting transfers between devices  11.3 us (7%)
  Pallas kernels  8.1 us (5%)
  local copies, waits for them, and re-layouts  8.04 us (5%)
  waiting for transfers between devices  3.91 us (2%)
  other arithmetic  3.33 us (2%)
    all_to_all x7, blocking collectives, exchange(): return lax.all_to_all(pieces, axes, 0, 0, tiled=True)  114 us
    all_to_all x1, starting transfers between devices, exchange(): return lax.all_to_all(pieces, axes, 0, 0, tiled=True)  11.3 us
    unnamed x11, local copies, waits for them, and re-layouts  7.08 us
    pallas_call x3, Pallas kernels, local_call(): pl.pallas_call(lambda *refs: kernel(slots, *refs), in_specs=[pl.BlockSpec...  5.86 us
    all_gather x2, blocking collectives, partner(): both = lax.all_gather(piece, 'core')  4.46 us
    all_gather x2, blocking collectives, shards(): lax.all_gather(spread(url_labels.astype(jnp.bfloat16), CHIPS), 'core')  4.34 us
    all_to_all x1, waiting for transfers between devices, exchange(): return lax.all_to_all(pieces, axes, 0, 0, tiled=True)  3.91 us
  transfers between devices with their start and end apart: 1, of which 1 were waited for; matrix products, arithmetic and copies ran while one was open for 1% of the time, Pallas kernels for 0%

profile of v4, /device:TPU:8, one launch (start us, length us, event | category | flops | bytes accessed | tf_op | source)
XLA Modules:
  0.0 159.3 jit_solution(9036976205208808546)
XLA Ops:
  0.6 0.8 convert_element_type.109
  1.4 0.7 broadcast_in_dim.22
  2.1 11.3 %all-to-all-start = ((bf16[16,64,128]{2,1,0:T(8,128)(2,1)}), bf16[16,64,128]{2,1,0:T(8,128)(2,1)S(1)}, u32[]{:S(2)}, u32[]{:S(2)}) async-start(bf16[16,64,128]{2,1,0:T(8,128)(2,1)} %broadcast_in_dim.22), calls=%async_computation | async-start | bytes 524288 | tf_op jit(solution)/shard_map/all_to_all | solution.py:160
  14.2 0.8 copy.14
  14.9 0.1 reshape.63
  15.0 0.1 pad_add_fusion.refs_0_
  15.1 0.0 copy-start.2
  15.1 2.2 %copy-done.2 = bf16[8,512,512]{2,1,0:T(8,128)(2,1)S(1)} copy-done((bf16[8,512,512]{2,1,0:T(8,128)(2,1)S(1)}, bf16[8,512,512]{2,1,0:T(8,128)(2,1)}, u32[]{:S(2)}) %copy-start.2) | copy-done | bytes 4194328
  17.3 0.0 copy-start.3
  17.3 0.0 copy-start.4
  17.3 0.3 shard_map.77.refs_2_
  17.6 0.0 copy-start
  17.6 1.9 %copy-done = bf16[8,512,512]{2,1,0:T(8,128)(2,1)} copy-done((bf16[8,512,512]{2,1,0:T(8,128)(2,1)}, bf16[8,512,512]{2,1,0:T(8,128)(2,1)S(1)}, u32[]{:S(2)}) %copy-start) | copy-done | bytes 4194328
  19.5 0.0 copy-done.3
  19.5 0.0 copy-done.4
  19.5 0.2 convolution_multiply_fusion
  19.7 3.9 %all-to-all-done.refs_1_ = bf16[16,64,128]{2,1,0:T(8,128)(2,1)S(1)} async-done(((bf16[16,64,128]{2,1,0:T(8,128)(2,1)}), bf16[16,64,128]{2,1,0:T(8,128)(2,1)S(1)}, u32[]{:S(2)}, u32[]{:S(2)}) %all-to-all-start) | async-done | bytes 262176 | tf_op jit(solution)/shard_map/all_to_all | solution.py:160
  23.6 0.0 copy-start.1
  23.6 2.2 %copy-done.1 = bf16[8,512,512]{2,1,0:T(8,128)(2,1)S(1)} copy-done((bf16[8,512,512]{2,1,0:T(8,128)(2,1)S(1)}, bf16[8,512,512]{2,1,0:T(8,128)(2,1)}, u32[]{:S(2)}) %copy-start.1) | copy-done | bytes 4194328
  25.8 1.8 %shard_map.78 = (f32[16,80,128]{2,1,0:T(8,128)S(1)}, f32[16,80,128]{2,1,0:T(8,128)S(1)}, bf16[8,512,512]{2,1,0:T(8,128)(2,1)S(1)}) custom-call(s32[18]{0:T(128)S(1)} %pad_add_fusion.refs_0_, bf16[16,64,128]{2,1,0:T(8,128)(2,1)S(1)} %all-to-all-done.refs_1_, bf16[8,512,512]{2,1,0:T(8,128)(2,1)S(1)} %copy-done.1), custom_call_target="tpu_custom_call", output_to_operand_aliasing={{2}: (2, {})} | custom-call | flops 268435456 | bytes 1048576 | tf_op jit(solution)/shard_map/pallas_call | solution.py:101
  27.7 0.1 multiply_convert_fusion.3
  27.8 0.1 fusion.8
  27.8 0.1 pad_maximum_fusion
  27.9 2.3 %all-gather = f16[32,80,128]{2,1,0:T(8,128)(2,1)S(1)} all-gather(f16[16,80,128]{2,1,0:T(8,128)(2,1)S(1)} %pad_maximum_fusion), channel_id=2, replica_groups=mesh['xh'=2,'y'=8,'core'=2,'xl'=2,'z'=8] {'core'}, dimensions={0}, use_global_device_ids=true | all-gather | bytes 983040 | tf_op jit(solution)/shard_map/all_gather | solution.py:169
  30.2 0.1 slice_select_fusion
  30.4 0.1 maximum_add_fusion
  30.6 0.1 fusion
  30.7 0.1 pad_maximum_fusion.1
  30.8 22.1 %all_to_all.40 = f16[16,67,128]{2,1,0:T(8,128)(2,1)S(1)} all-to-all(f16[16,67,128]{2,1,0:T(8,128)(2,1)S(1)} %pad_maximum_fusion.1), channel_id=1, replica_groups=mesh['xh'=2,'y'=8,'core'=2,'xl'=2,'z'=8] {'xh','y'}, dimensions={0} | all-to-all | bytes 548864 | tf_op jit(solution)/shard_map/all_to_all | solution.py:160
  53.0 0.1 multiply_reduce_fusion.3
  53.1 15.8 %all_to_all.41 = bf16[16,64,128]{2,1,0:T(8,128)(2,1)S(1)} all-to-all(bf16[16,64,128]{2,1,0:T(8,128)(2,1)S(1)} %broadcast_in_dim.46), channel_id=1, replica_groups=mesh['xh'=2,'y'=8,'core'=2,'xl'=2,'z'=8] {'xh','y'}, dimensions={0} | all-to-all | bytes 524288 | tf_op jit(solution)/shard_map/all_to_all | solution.py:160
  68.9 2.2 %all-gather.1 = bf16[32,64,128]{2,1,0:T(8,128)(2,1)S(1)} all-gather(bf16[16,64,128]{2,1,0:T(8,128)(2,1)S(1)} %all_to_all.41), channel_id=3, replica_groups=mesh['xh'=2,'y'=8,'core'=2,'xl'=2,'z'=8] {'core'}, dimensions={0}, use_global_device_ids=true | all-gather | bytes 786432 | tf_op jit(solution)/shard_map/all_gather | solution.py:231
  71.1 2.3 %shard_map.79 = (f32[16,80,128]{2,1,0:T(8,128)S(1)}, bf16[8,512,512]{2,1,0:T(8,128)(2,1)S(1)}) custom-call(s32[18]{0:T(128)S(1)} %pad_add_fusion.refs_0_, bf16[2,16,64,128]{3,2,1,0:T(8,128)(2,1)S(1)} %bitcast.10, bf16[8,512,512]{2,1,0:T(8,128)(2,1)S(1)} %get-tuple-element.21.refs_2_), custom_call_target="tpu_custom_call", output_to_operand_aliasing={{1}: (2, {})} | custom-call | flops 268435456 | bytes 1048576 | tf_op jit(solution)/shard_map/pallas_call | solution.py:101
  73.5 0.1 multiply_convert_fusion.2
  73.6 0.1 pad_maximum_fusion.2
  73.7 15.2 %all_to_all.42 = f16[16,67,128]{2,1,0:T(8,128)(2,1)S(1)} all-to-all(f16[16,67,128]{2,1,0:T(8,128)(2,1)S(1)} %pad_maximum_fusion.2), channel_id=1, replica_groups=mesh['xh'=2,'y'=8,'core'=2,'xl'=2,'z'=8] {'xl','z'}, dimensions={0} | all-to-all | bytes 548864 | tf_op jit(solution)/shard_map/all_to_all | solution.py:160
  89.0 0.1 multiply_reduce_fusion.2
  89.1 14.2 %all_to_all.43.refs_1_ = bf16[16,64,128]{2,1,0:T(8,128)(2,1)S(1)} all-to-all(bf16[16,64,128]{2,1,0:T(8,128)(2,1)S(1)} %broadcast_in_dim.47), channel_id=1, replica_groups=mesh['xh'=2,'y'=8,'core'=2,'xl'=2,'z'=8] {'xl','z'}, dimensions={0} | all-to-all | bytes 524288 | tf_op jit(solution)/shard_map/all_to_all | solution.py:160
  103.4 1.8 %shard_map.80 = (f32[16,64,128]{2,1,0:T(8,128)S(1)}, f32[16,64,128]{2,1,0:T(8,128)S(1)}, bf16[8,512,512]{2,1,0:T(8,128)(2,1)S(1)}) custom-call(s32[18]{0:T(128)S(1)} %pad_add_fusion.refs_0_, bf16[16,64,128]{2,1,0:T(8,128)(2,1)S(1)} %all_to_all.43.refs_1_, bf16[8,512,512]{2,1,0:T(8,128)(2,1)S(1)} %get-tuple-element.24.refs_2_), custom_call_target="tpu_custom_call", output_to_operand_aliasing={{2}: (2, {})} | custom-call | flops 268435456 | bytes 1048576 | tf_op jit(solution)/shard_map/pallas_call | solution.py:101
  105.2 0.1 multiply_convert_fusion.1
  105.2 2.2 %all-gather.2 = f16[32,64,128]{2,1,0:T(8,128)(2,1)S(1)} all-gather(f16[16,64,128]{2,1,0:T(8,128)(2,1)S(1)} %multiply_convert_fusion.1), channel_id=4, replica_groups=mesh['xh'=2,'y'=8,'core'=2,'xl'=2,'z'=8] {'core'}, dimensions={0}, use_global_device_ids=true | all-gather | bytes 786432 | tf_op jit(solution)/shard_map/all_gather | solution.py:169
  107.4 0.2 fusion.3
  107.6 16.3 %all_to_all.44 = f16[16,64,128]{2,1,0:T(8,128)(2,1)S(1)} all-to-all(f16[16,64,128]{2,1,0:T(8,128)(2,1)S(1)} %fusion.3), channel_id=1, replica_groups=mesh['xh'=2,'y'=8,'core'=2,'xl'=2,'z'=8] {'xh','y'}, dimensions={0} | all-to-all | bytes 524288 | tf_op jit(solution)/shard_map/all_to_all | solution.py:160
  123.9 0.1 multiply_reduce_fusion.1
  124.0 15.8 %all_to_all.45 = bf16[16,64,128]{2,1,0:T(8,128)(2,1)S(1)} all-to-all(bf16[16,64,128]{2,1,0:T(8,128)(2,1)S(1)} %broadcast_in_dim.48), channel_id=1, replica_groups=mesh['xh'=2,'y'=8,'core'=2,'xl'=2,'z'=8] {'xh','y'}, dimensions={0} | all-to-all | bytes 524288 | tf_op jit(solution)/shard_map/all_to_all | solution.py:160
  139.8 2.2 %all-gather.3 = bf16[32,64,128]{2,1,0:T(8,128)(2,1)S(1)} all-gather(bf16[16,64,128]{2,1,0:T(8,128)(2,1)S(1)} %all_to_all.45), channel_id=5, replica_groups=mesh['xh'=2,'y'=8,'core'=2,'xl'=2,'z'=8] {'core'}, dimensions={0}, use_global_device_ids=true | all-gather | bytes 786432 | tf_op jit(solution)/shard_map/all_gather | solution.py:231
  142.0 1.9 %shard_map.81 = (f32[16,64,128]{2,1,0:T(8,128)S(1)}, f32[64,128]{1,0:T(8,128)}) custom-call(s32[18]{0:T(128)S(1)} %pad_add_fusion.refs_0_, bf16[2,16,64,128]{3,2,1,0:T(8,128)(2,1)S(1)} %bitcast.9, bf16[8,512,512]{2,1,0:T(8,128)(2,1)S(1)} %get-tuple-element.27.refs_2_, f32[64,128]{1,0:T(8,128)S(1)} %get-tuple-element.31.refs_3_), custom_call_target="tpu_custom_call" | custom-call | flops 268435456 | bytes 1048576 | tf_op jit(solution)/shard_map/pallas_call | solution.py:116
  143.9 0.1 multiply_convert_fusion
  144.0 14.6 %all_to_all.46 = f16[16,64,128]{2,1,0:T(8,128)(2,1)S(1)} all-to-all(f16[16,64,128]{2,1,0:T(8,128)(2,1)S(1)} %multiply_convert_fusion), channel_id=1, replica_groups=mesh['xh'=2,'y'=8,'core'=2,'xl'=2,'z'=8] {'xl','z'}, dimensions={0} | all-to-all | bytes 524288 | tf_op jit(solution)/shard_map/all_to_all | solution.py:160
  158.6 0.1 multiply_reduce_fusion
  158.6 0.6 multiply_add_fusion
  (27 shorter events, 0.6 us)
Async XLA Ops:
  2.1 21.5 %all-to-all-start = ((bf16[16,64,128]{2,1,0:T(8,128)(2,1)}), bf16[16,64,128]{2,1,0:T(8,128)(2,1)S(1)}, u32[]{:S(2)}, u32[]{:S(2)}) async-start(bf16[16,64,128]{2,1,0:T(8,128)(2,1)} %broadcast_in_dim.22), calls=%async_computation | async-start | bytes 524288 | tf_op jit(solution)/shard_map/all_to_all | solution.py:160
  15.1 2.2 %copy-start.2 = (bf16[8,512,512]{2,1,0:T(8,128)(2,1)S(1)}, bf16[8,512,512]{2,1,0:T(8,128)(2,1)}, u32[]{:S(2)}) copy-start(bf16[8,512,512]{2,1,0:T(8,128)(2,1)} %source.1) | copy-start | bytes 12582916
  17.3 2.2 %copy-start.3 = (s32[32]{0:T(128)S(1)}, s32[32]{0:T(128)}, u32[]{:S(2)}) copy-start(s32[32]{0:T(128)} %param.10) | copy-start | bytes 388
  17.3 2.2 %copy-start.4 = (s32[32]{0:T(128)S(1)}, s32[32]{0:T(128)}, u32[]{:S(2)}) copy-start(s32[32]{0:T(128)} %param.11) | copy-start | bytes 388
  17.6 1.9 %copy-start = (bf16[8,512,512]{2,1,0:T(8,128)(2,1)}, bf16[8,512,512]{2,1,0:T(8,128)(2,1)S(1)}, u32[]{:S(2)}) copy-start(bf16[8,512,512]{2,1,0:T(8,128)(2,1)S(1)} %shard_map.77.refs_2_) | copy-start | bytes 12582916
  23.6 2.2 %copy-start.1 = (bf16[8,512,512]{2,1,0:T(8,128)(2,1)S(1)}, bf16[8,512,512]{2,1,0:T(8,128)(2,1)}, u32[]{:S(2)}) copy-start(bf16[8,512,512]{2,1,0:T(8,128)(2,1)} %copy-done) | copy-start | bytes 12582916

commit v5 on v2

--- a/solution.py
+++ b/solution.py
@@ -20,12 +20,6 @@
 COL = ("xl", "z")
 
 
-def load_kernel(source, loaded, sem):
-    copy = pltpu.make_async_copy(source, loaded, sem)
-    copy.start()
-    copy.wait()
-
-
 def widened(labels, rows, live):
     if rows > labels.shape[0]:
         ones = jnp.ones((rows - labels.shape[0], labels.shape[1]), labels.dtype)
@@ -37,7 +31,7 @@
     return (k < meta[2 * slots]).astype(jnp.float32).astype(jnp.bfloat16)
 
 
-def url_kernel(slots, meta, labels, tiles, own, other, kept):
+def url_kernel(slots, meta, labels, tiles, own, other):
     own[...] = jnp.zeros_like(own)
     other[...] = jnp.zeros_like(other)
     first = meta[2 * slots + 1] == 0
@@ -54,7 +48,7 @@
             other[2 * b + i] += jnp.where(first, odd, even)
 
 
-def query_kernel(slots, meta, labels, tiles, sums, kept):
+def query_kernel(slots, meta, labels, tiles, sums):
     sums[...] = jnp.zeros_like(sums)
     for k in range(slots):
         a = meta[2 * k]
@@ -66,31 +60,44 @@
             sums[4 * a + i] += term[:, i * LANES : (i + 1) * LANES]
 
 
+def last_kernel(slots, meta, labels, tiles, scores, sums, result, sem):
+    copy = pltpu.make_async_copy(scores, result, sem)
+    copy.start()
+    query_kernel(slots, meta, labels, tiles, sums)
+    copy.wait()
+
+
+COST = pl.CostEstimate(flops=2 * 64 * 512 * 512 * 8, bytes_accessed=1 << 20, transcendentals=0)
+
+
 def local_call(kernel, meta, labels, tiles, shapes):
     slots = tiles.shape[0]
     spec = pl.BlockSpec(memory_space=pltpu.VMEM)
-    sums = tuple(jax.ShapeDtypeStruct(shape, jnp.float32) for shape in shapes)
     return pl.pallas_call(
         lambda *refs: kernel(slots, *refs),
         in_specs=[pl.BlockSpec(memory_space=pltpu.SMEM), spec, spec],
-        out_specs=(spec,) * (len(sums) + 1),
-        out_shape=sums + (pltpu.VMEM(tiles.shape, tiles.dtype),),
-        input_output_aliases={2: len(sums)},
+        out_specs=(spec,) * len(shapes),
+        out_shape=tuple(jax.ShapeDtypeStruct(shape, jnp.float32) for shape in shapes),
         compiler_params=pltpu.CompilerParams(vmem_limit_bytes=VMEM_LIMIT),
-        cost_estimate=pl.CostEstimate(flops=2 * 64 * 512 * 512 * 8, bytes_accessed=1 << 20, transcendentals=0),
+        cost_estimate=COST,
     )(meta, labels, tiles)
 
 
-def load(tiles):
+def last_call(meta, labels, tiles, scores, shape):
+    slots = tiles.shape[0]
+    spec = pl.BlockSpec(memory_space=pltpu.VMEM)
     return pl.pallas_call(
-        load_kernel,
-        in_specs=[pl.BlockSpec(memory_space=pltpu.HBM)],
-        out_specs=pl.BlockSpec(memory_space=pltpu.VMEM),
-        out_shape=pltpu.VMEM(tiles.shape, tiles.dtype),
+        lambda *refs: last_kernel(slots, *refs),
+        in_specs=[pl.BlockSpec(memory_space=pltpu.SMEM), spec, spec, spec],
+        out_specs=(spec, pl.BlockSpec(memory_space=pl.ANY)),
+        out_shape=(
+            jax.ShapeDtypeStruct(shape, jnp.float32),
+            jax.ShapeDtypeStruct(scores.shape, scores.dtype),
+        ),
         scratch_shapes=[pltpu.SemaphoreType.DMA],
         compiler_params=pltpu.CompilerParams(vmem_limit_bytes=VMEM_LIMIT),
-        cost_estimate=pl.CostEstimate(flops=0, bytes_accessed=4 << 20, transcendentals=0),
-    )(tiles)
+        cost_estimate=COST,
+    )(meta, labels, tiles, scores)
 
 
 def inverse(degree):
@@ -171,19 +178,22 @@
     seeds = blend_rate * seed_weight * seed_map
 
     gathered = spread(prior_labels, COL)
-    tiles = load(click_tiles)
-    gathered, tiles, meta, seeds = lax.optimization_barrier((gathered, tiles, meta, seeds))
+    gathered, meta, seeds = lax.optimization_barrier((gathered, meta, seeds))
     core_known = url_known = query_known = None
     for iteration in range(ITERS):
         rows = classes + (EXTRA if iteration == 0 else 0)
         if iteration > 0:
             gathered = spread(labels.astype(jnp.bfloat16), COL)
         shape = (chip_count, rows, LANES)
-        own, other, tiles = local_call(url_kernel, meta, gathered, tiles, (shape, shape))
+        own, other = local_call(url_kernel, meta, gathered, click_tiles, (shape, shape))
         both, core_known = joined(own, other, classes, core == 0, core_known)
         url_labels, url_known = reduce(both, classes, CHIPS, url_known)
         both = lax.all_gather(spread(url_labels.astype(jnp.bfloat16), CHIPS), "core")
-        sums, tiles = local_call(query_kernel, meta, both, tiles, ((col_count, rows, LANES),))
+        shape = (col_count, rows, LANES)
+        if iteration < ITERS - 1:
+            (sums,) = local_call(query_kernel, meta, both, click_tiles, (shape,))
+        else:
+            sums, url_labels = last_call(meta, both, click_tiles, url_labels, shape)
         mean, query_known = reduce(sums, classes, COL, query_known)
         labels = (1.0 - blend_rate) * mean + seeds
     return labels, url_labels

time: 159 us -> 159 us (level)
  local copies, waits for them, and re-layouts: 8.04 us -> 3.91 us
  waiting for transfers between devices: 3.91 us -> 7.04 us
    unnamed x11 -> x5, local copies, waits for them, and re-layouts: 7.08 us -> 2.95 us
    all_to_all x1, waiting for transfers between devices: 3.91 us -> 7.04 us  [exchange(): return lax.all_to_all(pieces, axes, 0, 0, tiled=True)]
    pallas_call x4 -> x3, Pallas kernels: 6.73 us -> 4.71 us  [local_call(): pl.pallas_call(lambda *refs: kernel(slots, *refs), in_specs=[pl.BlockSpec...]
    pallas_call x1, Pallas kernels: 0.29 us -> 1.93 us  [last_call(): pl.pallas_call(lambda *refs: last_kernel(slots, *refs), in_specs=[pl.Bloc...]
  transfers between devices with their start and end apart: 1 -> 1, of which waited for: 1 -> 1; matrix products, arithmetic and copies ran while one was open for 1% -> 2% of each run, Pallas kernels for 0% -> 0%
where the time goes in v5:
time: 159 us; the launch traced here: 158 us
  blocking collectives  123 us (77%)
  starting transfers between devices  11.3 us (7%)
  waiting for transfers between devices  7.04 us (4%)
  Pallas kernels  6.65 us (4%)
  other arithmetic  3.99 us (3%)
  local copies, waits for them, and re-layouts  3.91 us (2%)
    all_to_all x7, blocking collectives, exchange(): return lax.all_to_all(pieces, axes, 0, 0, tiled=True)  114 us
    all_to_all x1, starting transfers between devices, exchange(): return lax.all_to_all(pieces, axes, 0, 0, tiled=True)  11.3 us
    all_to_all x1, waiting for transfers between devices, exchange(): return lax.all_to_all(pieces, axes, 0, 0, tiled=True)  7.04 us
    pallas_call x3, Pallas kernels, local_call(): pl.pallas_call(lambda *refs: kernel(slots, *refs), in_specs=[pl.BlockSpec...  4.71 us
    all_gather x2, blocking collectives, partner(): both = lax.all_gather(piece, 'core')  4.59 us
    all_gather x2, blocking collectives, shards(): lax.all_gather(spread(url_labels.astype(jnp.bfloat16), CHIPS), 'core')  4.34 us
  transfers between devices with their start and end apart: 1, of which 1 were waited for; matrix products, arithmetic and copies ran while one was open for 2% of the time, Pallas kernels for 0%

profile of v5, /device:TPU:8, one launch (start us, length us, event | category | flops | bytes accessed | tf_op | source)
XLA Modules:
  0.0 158.2 jit_solution(3389797999266492716)
XLA Ops:
  0.6 0.8 convert_element_type.109
  1.4 0.7 broadcast_in_dim.22
  2.1 11.3 %all-to-all-start = ((bf16[16,64,128]{2,1,0:T(8,128)(2,1)}), bf16[16,64,128]{2,1,0:T(8,128)(2,1)S(1)}, u32[]{:S(2)}, u32[]{:S(2)}) async-start(bf16[16,64,128]{2,1,0:T(8,128)(2,1)} %broadcast_in_dim.22), calls=%async_computation | async-start | bytes 524288 | tf_op jit(solution)/shard_map/all_to_all | solution.py:121
  14.1 0.8 copy.11
  14.9 0.1 reshape.63
  15.0 0.1 pad_add_fusion.refs_0_
  15.1 0.7 broadcast_subtract_fusion
  15.7 0.8 convolution_multiply_fusion
  16.6 7.0 %all-to-all-done.refs_1_ = bf16[16,64,128]{2,1,0:T(8,128)(2,1)S(1)} async-done(((bf16[16,64,128]{2,1,0:T(8,128)(2,1)}), bf16[16,64,128]{2,1,0:T(8,128)(2,1)S(1)}, u32[]{:S(2)}, u32[]{:S(2)}) %all-to-all-start) | async-done | bytes 262176 | tf_op jit(solution)/shard_map/all_to_all | solution.py:121
  23.6 0.0 copy-start
  23.6 2.2 %copy-done = bf16[8,512,512]{2,1,0:T(8,128)(2,1)S(1)} copy-done((bf16[8,512,512]{2,1,0:T(8,128)(2,1)S(1)}, bf16[8,512,512]{2,1,0:T(8,128)(2,1)}, u32[]{:S(2)}) %copy-start) | copy-done | bytes 4194328
  25.8 1.4 shard_map.77
  27.3 0.1 multiply_convert_fusion.2
  27.4 0.1 fusion.9
  27.4 0.1 pad_maximum_fusion
  27.5 0.0 copy-start.1
  27.5 2.4 %all-gather = f16[32,80,128]{2,1,0:T(8,128)(2,1)S(1)} all-gather(f16[16,80,128]{2,1,0:T(8,128)(2,1)S(1)} %pad_maximum_fusion), channel_id=2, replica_groups=mesh['xh'=2,'y'=8,'core'=2,'xl'=2,'z'=8] {'core'}, dimensions={0}, use_global_device_ids=true | all-gather | bytes 983040 | tf_op jit(solution)/shard_map/all_gather | solution.py:130
  30.0 0.1 slice_select_fusion
  30.2 0.1 maximum_add_fusion
  30.3 0.1 fusion.1
  30.4 0.1 pad_maximum_fusion.1
  30.6 22.1 %all_to_all.40 = f16[16,67,128]{2,1,0:T(8,128)(2,1)S(1)} all-to-all(f16[16,67,128]{2,1,0:T(8,128)(2,1)S(1)} %pad_maximum_fusion.1), channel_id=1, replica_groups=mesh['xh'=2,'y'=8,'core'=2,'xl'=2,'z'=8] {'xh','y'}, dimensions={0} | all-to-all | bytes 548864 | tf_op jit(solution)/shard_map/all_to_all | solution.py:121
  52.8 0.1 multiply_reduce_fusion.3
  52.9 15.8 %all_to_all.41 = bf16[16,64,128]{2,1,0:T(8,128)(2,1)S(1)} all-to-all(bf16[16,64,128]{2,1,0:T(8,128)(2,1)S(1)} %broadcast_in_dim.46), channel_id=1, replica_groups=mesh['xh'=2,'y'=8,'core'=2,'xl'=2,'z'=8] {'xh','y'}, dimensions={0} | all-to-all | bytes 524288 | tf_op jit(solution)/shard_map/all_to_all | solution.py:121
  68.7 2.2 %all-gather.1 = bf16[32,64,128]{2,1,0:T(8,128)(2,1)S(1)} all-gather(bf16[16,64,128]{2,1,0:T(8,128)(2,1)S(1)} %all_to_all.41), channel_id=3, replica_groups=mesh['xh'=2,'y'=8,'core'=2,'xl'=2,'z'=8] {'core'}, dimensions={0}, use_global_device_ids=true | all-gather | bytes 786432 | tf_op jit(solution)/shard_map/all_gather | solution.py:191
  70.9 0.0 copy-done.1
  70.9 1.9 %shard_map.78 = f32[16,80,128]{2,1,0:T(8,128)S(1)} custom-call(s32[18]{0:T(128)S(1)} %pad_add_fusion.refs_0_, bf16[2,16,64,128]{3,2,1,0:T(8,128)(2,1)S(1)} %bitcast.10, bf16[8,512,512]{2,1,0:T(8,128)(2,1)S(1)} %copy-done.1), custom_call_target="tpu_custom_call" | custom-call | flops 268435456 | bytes 1048576 | tf_op jit(solution)/shard_map/pallas_call | solution.py:76
  72.9 0.1 fusion
  73.0 0.1 pad_maximum_fusion.2
  73.1 15.2 %all_to_all.42 = f16[16,67,128]{2,1,0:T(8,128)(2,1)S(1)} all-to-all(f16[16,67,128]{2,1,0:T(8,128)(2,1)S(1)} %pad_maximum_fusion.2), channel_id=1, replica_groups=mesh['xh'=2,'y'=8,'core'=2,'xl'=2,'z'=8] {'xl','z'}, dimensions={0} | all-to-all | bytes 548864 | tf_op jit(solution)/shard_map/all_to_all | solution.py:121
  88.4 0.1 multiply_reduce_fusion.2
  88.5 14.2 %all_to_all.43.refs_1_ = bf16[16,64,128]{2,1,0:T(8,128)(2,1)S(1)} all-to-all(bf16[16,64,128]{2,1,0:T(8,128)(2,1)S(1)} %broadcast_in_dim.47), channel_id=1, replica_groups=mesh['xh'=2,'y'=8,'core'=2,'xl'=2,'z'=8] {'xl','z'}, dimensions={0} | all-to-all | bytes 524288 | tf_op jit(solution)/shard_map/all_to_all | solution.py:121
  102.8 1.4 shard_map.79
  104.1 0.1 multiply_convert_fusion.1
  104.2 2.2 %all-gather.2 = f16[32,64,128]{2,1,0:T(8,128)(2,1)S(1)} all-gather(f16[16,64,128]{2,1,0:T(8,128)(2,1)S(1)} %multiply_convert_fusion.1), channel_id=4, replica_groups=mesh['xh'=2,'y'=8,'core'=2,'xl'=2,'z'=8] {'core'}, dimensions={0}, use_global_device_ids=true | all-gather | bytes 786432 | tf_op jit(solution)/shard_map/all_gather | solution.py:130
  106.4 0.2 fusion.4
  106.6 16.3 %all_to_all.44 = f16[16,64,128]{2,1,0:T(8,128)(2,1)S(1)} all-to-all(f16[16,64,128]{2,1,0:T(8,128)(2,1)S(1)} %fusion.4), channel_id=1, replica_groups=mesh['xh'=2,'y'=8,'core'=2,'xl'=2,'z'=8] {'xh','y'}, dimensions={0} | all-to-all | bytes 524288 | tf_op jit(solution)/shard_map/all_to_all | solution.py:121
  122.9 0.1 multiply_reduce_fusion.1
  123.0 15.8 %all_to_all.45 = bf16[16,64,128]{2,1,0:T(8,128)(2,1)S(1)} all-to-all(bf16[16,64,128]{2,1,0:T(8,128)(2,1)S(1)} %broadcast_in_dim.48), channel_id=1, replica_groups=mesh['xh'=2,'y'=8,'core'=2,'xl'=2,'z'=8] {'xh','y'}, dimensions={0} | all-to-all | bytes 524288 | tf_op jit(solution)/shard_map/all_to_all | solution.py:121
  138.8 2.2 %all-gather.3 = bf16[32,64,128]{2,1,0:T(8,128)(2,1)S(1)} all-gather(bf16[16,64,128]{2,1,0:T(8,128)(2,1)S(1)} %all_to_all.45), channel_id=5, replica_groups=mesh['xh'=2,'y'=8,'core'=2,'xl'=2,'z'=8] {'core'}, dimensions={0}, use_global_device_ids=true | all-gather | bytes 786432 | tf_op jit(solution)/shard_map/all_gather | solution.py:191
  141.0 1.9 %shard_map.80 = (f32[16,64,128]{2,1,0:T(8,128)S(1)}, f32[64,128]{1,0:T(8,128)}) custom-call(s32[18]{0:T(128)S(1)} %pad_add_fusion.refs_0_, bf16[2,16,64,128]{3,2,1,0:T(8,128)(2,1)S(1)} %bitcast.9, bf16[8,512,512]{2,1,0:T(8,128)(2,1)S(1)} %copy-done.1, f32[64,128]{1,0:T(8,128)S(1)} %get-tuple-element.21.refs_3_), custom_call_target="tpu_custom_call" | custom-call | flops 268435456 | bytes 1048576 | tf_op jit(solution)/shard_map/pallas_call | solution.py:89
  142.9 0.1 multiply_convert_fusion
  143.0 14.6 %all_to_all.46 = f16[16,64,128]{2,1,0:T(8,128)(2,1)S(1)} all-to-all(f16[16,64,128]{2,1,0:T(8,128)(2,1)S(1)} %multiply_convert_fusion), channel_id=1, replica_groups=mesh['xh'=2,'y'=8,'core'=2,'xl'=2,'z'=8] {'xl','z'}, dimensions={0} | all-to-all | bytes 524288 | tf_op jit(solution)/shard_map/all_to_all | solution.py:121
  157.5 0.1 multiply_reduce_fusion
  157.6 0.6 multiply_add_fusion
  (26 shorter events, 0.6 us)
Async XLA Ops:
  2.1 21.5 %all-to-all-start = ((bf16[16,64,128]{2,1,0:T(8,128)(2,1)}), bf16[16,64,128]{2,1,0:T(8,128)(2,1)S(1)}, u32[]{:S(2)}, u32[]{:S(2)}) async-start(bf16[16,64,128]{2,1,0:T(8,128)(2,1)} %broadcast_in_dim.22), calls=%async_computation | async-start | bytes 524288 | tf_op jit(solution)/shard_map/all_to_all | solution.py:121
  23.6 2.2 %copy-start = (bf16[8,512,512]{2,1,0:T(8,128)(2,1)S(1)}, bf16[8,512,512]{2,1,0:T(8,128)(2,1)}, u32[]{:S(2)}) copy-start(bf16[8,512,512]{2,1,0:T(8,128)(2,1)} %refs_2_.7) | copy-start | bytes 12582916
  27.5 43.3 %copy-start.1 = (bf16[8,512,512]{2,1,0:T(8,128)(2,1)S(1)}, bf16[8,512,512]{2,1,0:T(8,128)(2,1)}, u32[]{:S(2)}) copy-start(bf16[8,512,512]{2,1,0:T(8,128)(2,1)} %refs_2_.7) | copy-start | bytes 12582916

commit v6 on v5

--- a/solution.py
+++ b/solution.py
@@ -11,6 +11,7 @@
 LANES = 128
 EXTRA = 16
 SCALE = 512.0
+LEAST = 1e-30
 VMEM_LIMIT = 16 * 1024 * 1024
 
 blend_rate = 0.25
@@ -100,12 +101,8 @@
     )(meta, labels, tiles, scores)
 
 
-def inverse(degree):
-    return jnp.where(degree > 0.0, SCALE / jnp.where(degree > 0.0, degree, 1.0), 0.0)
-
-
 def degree_rows(degree):
-    power = jnp.where(degree > 0.0, jnp.floor(jnp.log2(jnp.maximum(degree, 1e-30))), 0.0)
+    power = jnp.floor(jnp.log2(degree))
     part = degree * jnp.exp2(-power)
     high = part.astype(jnp.float16)
     low = (part - high.astype(jnp.float32)).astype(jnp.float16)
@@ -133,8 +130,8 @@
 
 def joined(own, other, classes, first, known):
     if known is None:
-        degree = other[:, classes : classes + 1]
-        scale = inverse(degree)
+        degree = jnp.maximum(other[:, classes : classes + 1], LEAST)
+        scale = SCALE / degree
         rest = degree_rows(degree)
         rest = jnp.pad(rest, ((0, 0), (0, EXTRA - rest.shape[1]), (0, 0)))
         arrived = partner(jnp.concatenate([(other[:, :classes] * scale).astype(jnp.float16), rest], axis=1), first)
@@ -149,8 +146,8 @@
 
 def reduce(sums, classes, axes, known):
     if known is None:
-        degree = sums[:, classes : classes + 1]
-        scale = inverse(degree)
+        degree = jnp.maximum(sums[:, classes : classes + 1], LEAST)
+        scale = SCALE / degree
         message = jnp.concatenate([(sums[:, :classes] * scale).astype(jnp.float16), degree_rows(degree)], axis=1)
         arrived = exchange(message, axes)
         weights = degree_of(arrived[:, classes:])

time: 159 us -> 159 us (level)
  no operation moved by 1% of the time
where the time goes in v6:
time: 159 us; the launch traced here: 158 us
  blocking collectives  123 us (77%)
  starting transfers between devices  11.3 us (7%)
  waiting for transfers between devices  7.04 us (4%)
  Pallas kernels  6.65 us (4%)
  other arithmetic  3.96 us (2%)
  local copies, waits for them, and re-layouts  3.91 us (2%)
    all_to_all x7, blocking collectives, exchange(): return lax.all_to_all(pieces, axes, 0, 0, tiled=True)  114 us
    all_to_all x1, starting transfers between devices, exchange(): return lax.all_to_all(pieces, axes, 0, 0, tiled=True)  11.3 us
    all_to_all x1, waiting for transfers between devices, exchange(): return lax.all_to_all(pieces, axes, 0, 0, tiled=True)  7.04 us
    pallas_call x3, Pallas kernels, local_call(): pl.pallas_call(lambda *refs: kernel(slots, *refs), in_specs=[pl.BlockSpec...  4.71 us
    all_gather x2, blocking collectives, partner(): both = lax.all_gather(piece, 'core')  4.59 us
    all_gather x2, blocking collectives, shards(): lax.all_gather(spread(url_labels.astype(jnp.bfloat16), CHIPS), 'core')  4.34 us
  transfers between devices with their start and end apart: 1, of which 1 were waited for; matrix products, arithmetic and copies ran while one was open for 2% of the time, Pallas kernels for 0%

profile of v6, /device:TPU:8, one launch (start us, length us, event | category | flops | bytes accessed | tf_op | source)
XLA Modules:
  0.0 158.2 jit_solution(9215251088344557167)
XLA Ops:
  0.6 0.8 convert_element_type.109
  1.4 0.7 broadcast_in_dim.10
  2.1 11.3 %all-to-all-start = ((bf16[16,64,128]{2,1,0:T(8,128)(2,1)}), bf16[16,64,128]{2,1,0:T(8,128)(2,1)S(1)}, u32[]{:S(2)}, u32[]{:S(2)}) async-start(bf16[16,64,128]{2,1,0:T(8,128)(2,1)} %broadcast_in_dim.10), calls=%async_computation | async-start | bytes 524288 | tf_op jit(solution)/shard_map/all_to_all | solution.py:118
  14.1 0.8 copy.11
  14.9 0.1 reshape.63
  15.0 0.1 pad_add_fusion.refs_0_
  15.1 0.7 broadcast_subtract_fusion
  15.7 0.8 convolution_multiply_fusion
  16.6 7.0 %all-to-all-done.refs_1_ = bf16[16,64,128]{2,1,0:T(8,128)(2,1)S(1)} async-done(((bf16[16,64,128]{2,1,0:T(8,128)(2,1)}), bf16[16,64,128]{2,1,0:T(8,128)(2,1)S(1)}, u32[]{:S(2)}, u32[]{:S(2)}) %all-to-all-start) | async-done | bytes 262176 | tf_op jit(solution)/shard_map/all_to_all | solution.py:118
  23.6 0.0 copy-start
  23.6 2.2 %copy-done = bf16[8,512,512]{2,1,0:T(8,128)(2,1)S(1)} copy-done((bf16[8,512,512]{2,1,0:T(8,128)(2,1)S(1)}, bf16[8,512,512]{2,1,0:T(8,128)(2,1)}, u32[]{:S(2)}) %copy-start) | copy-done | bytes 4194328
  25.8 1.4 shard_map.77
  27.2 0.1 fusion.21
  27.3 0.1 multiply_convert_fusion.2
  27.4 0.1 fusion.9
  27.4 0.1 pad_maximum_fusion
  27.5 0.0 copy-start.1
  27.5 2.4 %all-gather = f16[32,80,128]{2,1,0:T(8,128)(2,1)S(1)} all-gather(f16[16,80,128]{2,1,0:T(8,128)(2,1)S(1)} %pad_maximum_fusion), channel_id=2, replica_groups=mesh['xh'=2,'y'=8,'core'=2,'xl'=2,'z'=8] {'core'}, dimensions={0}, use_global_device_ids=true | all-gather | bytes 983040 | tf_op jit(solution)/shard_map/all_gather | solution.py:127
  29.9 0.1 slice_select_fusion
  30.2 0.1 maximum_add_fusion
  30.3 0.1 fusion.22
  30.3 0.1 fusion.1
  30.4 0.1 pad_maximum_fusion.1
  30.6 22.1 %all_to_all.40 = f16[16,67,128]{2,1,0:T(8,128)(2,1)S(1)} all-to-all(f16[16,67,128]{2,1,0:T(8,128)(2,1)S(1)} %pad_maximum_fusion.1), channel_id=1, replica_groups=mesh['xh'=2,'y'=8,'core'=2,'xl'=2,'z'=8] {'xh','y'}, dimensions={0} | all-to-all | bytes 548864 | tf_op jit(solution)/shard_map/all_to_all | solution.py:118
  52.7 0.1 multiply_reduce_fusion.3
  52.9 15.8 %all_to_all.41 = bf16[16,64,128]{2,1,0:T(8,128)(2,1)S(1)} all-to-all(bf16[16,64,128]{2,1,0:T(8,128)(2,1)S(1)} %broadcast_in_dim.12), channel_id=1, replica_groups=mesh['xh'=2,'y'=8,'core'=2,'xl'=2,'z'=8] {'xh','y'}, dimensions={0} | all-to-all | bytes 524288 | tf_op jit(solution)/shard_map/all_to_all | solution.py:118
  68.7 2.2 %all-gather.1 = bf16[32,64,128]{2,1,0:T(8,128)(2,1)S(1)} all-gather(bf16[16,64,128]{2,1,0:T(8,128)(2,1)S(1)} %all_to_all.41), channel_id=3, replica_groups=mesh['xh'=2,'y'=8,'core'=2,'xl'=2,'z'=8] {'core'}, dimensions={0}, use_global_device_ids=true | all-gather | bytes 786432 | tf_op jit(solution)/shard_map/all_gather | solution.py:188
  70.8 0.0 copy-done.1
  70.8 1.9 %shard_map.78 = f32[16,80,128]{2,1,0:T(8,128)S(1)} custom-call(s32[18]{0:T(128)S(1)} %pad_add_fusion.refs_0_, bf16[2,16,64,128]{3,2,1,0:T(8,128)(2,1)S(1)} %bitcast.13, bf16[8,512,512]{2,1,0:T(8,128)(2,1)S(1)} %copy-done.1), custom_call_target="tpu_custom_call" | custom-call | flops 268435456 | bytes 1048576 | tf_op jit(solution)/shard_map/pallas_call | solution.py:77
  72.8 0.1 fusion.23
  72.8 0.1 fusion
  72.9 0.1 pad_maximum_fusion.2
  73.1 15.2 %all_to_all.42 = f16[16,67,128]{2,1,0:T(8,128)(2,1)S(1)} all-to-all(f16[16,67,128]{2,1,0:T(8,128)(2,1)S(1)} %pad_maximum_fusion.2), channel_id=1, replica_groups=mesh['xh'=2,'y'=8,'core'=2,'xl'=2,'z'=8] {'xl','z'}, dimensions={0} | all-to-all | bytes 548864 | tf_op jit(solution)/shard_map/all_to_all | solution.py:118
  88.3 0.1 multiply_reduce_fusion.2
  88.5 14.2 %all_to_all.43.refs_1_ = bf16[16,64,128]{2,1,0:T(8,128)(2,1)S(1)} all-to-all(bf16[16,64,128]{2,1,0:T(8,128)(2,1)S(1)} %broadcast_in_dim.13), channel_id=1, replica_groups=mesh['xh'=2,'y'=8,'core'=2,'xl'=2,'z'=8] {'xl','z'}, dimensions={0} | all-to-all | bytes 524288 | tf_op jit(solution)/shard_map/all_to_all | solution.py:118
  102.7 1.4 shard_map.79
  104.1 0.1 multiply_convert_fusion.1
  104.2 2.2 %all-gather.2 = f16[32,64,128]{2,1,0:T(8,128)(2,1)S(1)} all-gather(f16[16,64,128]{2,1,0:T(8,128)(2,1)S(1)} %multiply_convert_fusion.1), channel_id=4, replica_groups=mesh['xh'=2,'y'=8,'core'=2,'xl'=2,'z'=8] {'core'}, dimensions={0}, use_global_device_ids=true | all-gather | bytes 786432 | tf_op jit(solution)/shard_map/all_gather | solution.py:127
  106.4 0.2 fusion.4
  106.5 16.3 %all_to_all.44 = f16[16,64,128]{2,1,0:T(8,128)(2,1)S(1)} all-to-all(f16[16,64,128]{2,1,0:T(8,128)(2,1)S(1)} %fusion.4), channel_id=1, replica_groups=mesh['xh'=2,'y'=8,'core'=2,'xl'=2,'z'=8] {'xh','y'}, dimensions={0} | all-to-all | bytes 524288 | tf_op jit(solution)/shard_map/all_to_all | solution.py:118
  122.8 0.1 multiply_reduce_fusion.1
  122.9 15.8 %all_to_all.45 = bf16[16,64,128]{2,1,0:T(8,128)(2,1)S(1)} all-to-all(bf16[16,64,128]{2,1,0:T(8,128)(2,1)S(1)} %broadcast_in_dim.14), channel_id=1, replica_groups=mesh['xh'=2,'y'=8,'core'=2,'xl'=2,'z'=8] {'xh','y'}, dimensions={0} | all-to-all | bytes 524288 | tf_op jit(solution)/shard_map/all_to_all | solution.py:118
  138.8 2.2 %all-gather.3 = bf16[32,64,128]{2,1,0:T(8,128)(2,1)S(1)} all-gather(bf16[16,64,128]{2,1,0:T(8,128)(2,1)S(1)} %all_to_all.45), channel_id=5, replica_groups=mesh['xh'=2,'y'=8,'core'=2,'xl'=2,'z'=8] {'core'}, dimensions={0}, use_global_device_ids=true | all-gather | bytes 786432 | tf_op jit(solution)/shard_map/all_gather | solution.py:188
  140.9 1.9 %shard_map.80 = (f32[16,64,128]{2,1,0:T(8,128)S(1)}, f32[64,128]{1,0:T(8,128)}) custom-call(s32[18]{0:T(128)S(1)} %pad_add_fusion.refs_0_, bf16[2,16,64,128]{3,2,1,0:T(8,128)(2,1)S(1)} %bitcast.12, bf16[8,512,512]{2,1,0:T(8,128)(2,1)S(1)} %copy-done.1, f32[64,128]{1,0:T(8,128)S(1)} %get-tuple-element.21.refs_3_), custom_call_target="tpu_custom_call" | custom-call | flops 268435456 | bytes 1048576 | tf_op jit(solution)/shard_map/pallas_call | solution.py:90
  142.9 0.1 multiply_convert_fusion
  142.9 14.6 %all_to_all.46 = f16[16,64,128]{2,1,0:T(8,128)(2,1)S(1)} all-to-all(f16[16,64,128]{2,1,0:T(8,128)(2,1)S(1)} %multiply_convert_fusion), channel_id=1, replica_groups=mesh['xh'=2,'y'=8,'core'=2,'xl'=2,'z'=8] {'xl','z'}, dimensions={0} | all-to-all | bytes 524288 | tf_op jit(solution)/shard_map/all_to_all | solution.py:118
  157.5 0.1 multiply_reduce_fusion
  157.6 0.6 multiply_add_fusion
  (21 shorter events, 0.4 us)
Async XLA Ops:
  2.1 21.5 %all-to-all-start = ((bf16[16,64,128]{2,1,0:T(8,128)(2,1)}), bf16[16,64,128]{2,1,0:T(8,128)(2,1)S(1)}, u32[]{:S(2)}, u32[]{:S(2)}) async-start(bf16[16,64,128]{2,1,0:T(8,128)(2,1)} %broadcast_in_dim.10), calls=%async_computation | async-start | bytes 524288 | tf_op jit(solution)/shard_map/all_to_all | solution.py:118
  23.6 2.2 %copy-start = (bf16[8,512,512]{2,1,0:T(8,128)(2,1)S(1)}, bf16[8,512,512]{2,1,0:T(8,128)(2,1)}, u32[]{:S(2)}) copy-start(bf16[8,512,512]{2,1,0:T(8,128)(2,1)} %refs_2_.7) | copy-start | bytes 12582916
  27.5 43.3 %copy-start.1 = (bf16[8,512,512]{2,1,0:T(8,128)(2,1)S(1)}, bf16[8,512,512]{2,1,0:T(8,128)(2,1)}, u32[]{:S(2)}) copy-start(bf16[8,512,512]{2,1,0:T(8,128)(2,1)} %refs_2_.7) | copy-start | bytes 12582916

commit v7 on v6

--- a/solution.py
+++ b/solution.py
@@ -174,7 +174,8 @@
     seed_map = jnp.dot(class_onehot, place_onehot, preferred_element_type=jnp.float32)
     seeds = blend_rate * seed_weight * seed_map
 
-    gathered = spread(prior_labels, COL)
+    copies = jnp.arange(col_count)[:, None, None] - core < col_count
+    gathered = exchange(jnp.where(copies, prior_labels[None], 0.0).astype(jnp.bfloat16), COL)
     gathered, meta, seeds = lax.optimization_barrier((gathered, meta, seeds))
     core_known = url_known = query_known = None
     for iteration in range(ITERS):

time: 159 us -> 159 us (level)
  no operation moved by 1% of the time
where the time goes in v7:
time: 159 us; the launch traced here: 158 us
  blocking collectives  123 us (77%)
  starting transfers between devices  11.3 us (7%)
  waiting for transfers between devices  7.04 us (4%)
  Pallas kernels  6.65 us (4%)
  other arithmetic  4.77 us (3%)
  local copies, waits for them, and re-layouts  3.16 us (2%)
    all_to_all x7, blocking collectives, exchange(): return lax.all_to_all(pieces, axes, 0, 0, tiled=True)  114 us
    all_to_all x1, starting transfers between devices, exchange(): return lax.all_to_all(pieces, axes, 0, 0, tiled=True)  11.3 us
    all_to_all x1, waiting for transfers between devices, exchange(): return lax.all_to_all(pieces, axes, 0, 0, tiled=True)  7.04 us
    pallas_call x3, Pallas kernels, local_call(): pl.pallas_call(lambda *refs: kernel(slots, *refs), in_specs=[pl.BlockSpec...  4.72 us
    all_gather x2, blocking collectives, partner(): both = lax.all_gather(piece, 'core')  4.59 us
    all_gather x2, blocking collectives, shards(): lax.all_gather(spread(url_labels.astype(jnp.bfloat16), CHIPS), 'core')  4.34 us
  transfers between devices with their start and end apart: 1, of which 1 were waited for; matrix products, arithmetic and copies ran while one was open for 2% of the time, Pallas kernels for 0%

profile of v7, /device:TPU:8, one launch (start us, length us, event | category | flops | bytes accessed | tf_op | source)
XLA Modules:
  0.0 158.3 jit_solution(13059360820195147627)
XLA Ops:
  0.6 1.6 select_convert_fusion
  2.2 11.3 %all-to-all-start = ((bf16[16,64,128]{2,1,0:T(8,128)(2,1)}), bf16[16,64,128]{2,1,0:T(8,128)(2,1)S(1)}, u32[]{:S(2)}, u32[]{:S(2)}) async-start(bf16[16,64,128]{2,1,0:T(8,128)(2,1)} %select_convert_fusion), calls=%async_computation | async-start | bytes 524288 | tf_op jit(solution)/shard_map/all_to_all | solution.py:118
  14.2 0.8 copy.11
  15.0 0.1 reshape.70
  15.0 0.1 pad_add_fusion.refs_0_
  15.1 0.7 broadcast_subtract_fusion
  15.8 0.8 convolution_multiply_fusion
  16.6 7.0 %all-to-all-done.refs_1_ = bf16[16,64,128]{2,1,0:T(8,128)(2,1)S(1)} async-done(((bf16[16,64,128]{2,1,0:T(8,128)(2,1)}), bf16[16,64,128]{2,1,0:T(8,128)(2,1)S(1)}, u32[]{:S(2)}, u32[]{:S(2)}) %all-to-all-start) | async-done | bytes 262176 | tf_op jit(solution)/shard_map/all_to_all | solution.py:118
  23.7 0.0 copy-start
  23.7 2.2 %copy-done = bf16[8,512,512]{2,1,0:T(8,128)(2,1)S(1)} copy-done((bf16[8,512,512]{2,1,0:T(8,128)(2,1)S(1)}, bf16[8,512,512]{2,1,0:T(8,128)(2,1)}, u32[]{:S(2)}) %copy-start) | copy-done | bytes 4194328
  25.9 1.4 shard_map.77
  27.3 0.1 fusion.21
  27.4 0.1 multiply_convert_fusion.2
  27.4 0.1 fusion.9
  27.5 0.1 pad_maximum_fusion
  27.6 0.0 copy-start.1
  27.6 2.4 %all-gather = f16[32,80,128]{2,1,0:T(8,128)(2,1)S(1)} all-gather(f16[16,80,128]{2,1,0:T(8,128)(2,1)S(1)} %pad_maximum_fusion), channel_id=2, replica_groups=mesh['xh'=2,'y'=8,'core'=2,'xl'=2,'z'=8] {'core'}, dimensions={0}, use_global_device_ids=true | all-gather | bytes 983040 | tf_op jit(solution)/shard_map/all_gather | solution.py:127
  30.0 0.1 slice_select_fusion
  30.2 0.1 maximum_add_fusion
  30.3 0.1 fusion.22
  30.4 0.1 fusion.1
  30.5 0.1 pad_maximum_fusion.1
  30.6 22.1 %all_to_all.40 = f16[16,67,128]{2,1,0:T(8,128)(2,1)S(1)} all-to-all(f16[16,67,128]{2,1,0:T(8,128)(2,1)S(1)} %pad_maximum_fusion.1), channel_id=1, replica_groups=mesh['xh'=2,'y'=8,'core'=2,'xl'=2,'z'=8] {'xh','y'}, dimensions={0} | all-to-all | bytes 548864 | tf_op jit(solution)/shard_map/all_to_all | solution.py:118
  52.8 0.1 multiply_reduce_fusion.3
  52.9 15.8 %all_to_all.41 = bf16[16,64,128]{2,1,0:T(8,128)(2,1)S(1)} all-to-all(bf16[16,64,128]{2,1,0:T(8,128)(2,1)S(1)} %broadcast_in_dim.32), channel_id=1, replica_groups=mesh['xh'=2,'y'=8,'core'=2,'xl'=2,'z'=8] {'xh','y'}, dimensions={0} | all-to-all | bytes 524288 | tf_op jit(solution)/shard_map/all_to_all | solution.py:118
  68.7 2.2 %all-gather.1 = bf16[32,64,128]{2,1,0:T(8,128)(2,1)S(1)} all-gather(bf16[16,64,128]{2,1,0:T(8,128)(2,1)S(1)} %all_to_all.41), channel_id=3, replica_groups=mesh['xh'=2,'y'=8,'core'=2,'xl'=2,'z'=8] {'core'}, dimensions={0}, use_global_device_ids=true | all-gather | bytes 786432 | tf_op jit(solution)/shard_map/all_gather | solution.py:189
  70.9 0.0 copy-done.1
  70.9 1.9 %shard_map.78 = f32[16,80,128]{2,1,0:T(8,128)S(1)} custom-call(s32[18]{0:T(128)S(1)} %pad_add_fusion.refs_0_, bf16[2,16,64,128]{3,2,1,0:T(8,128)(2,1)S(1)} %bitcast.13, bf16[8,512,512]{2,1,0:T(8,128)(2,1)S(1)} %copy-done.1), custom_call_target="tpu_custom_call" | custom-call | flops 268435456 | bytes 1048576 | tf_op jit(solution)/shard_map/pallas_call | solution.py:77
  72.8 0.1 fusion.23
  72.9 0.1 fusion
  73.0 0.1 pad_maximum_fusion.2
  73.1 15.2 %all_to_all.42 = f16[16,67,128]{2,1,0:T(8,128)(2,1)S(1)} all-to-all(f16[16,67,128]{2,1,0:T(8,128)(2,1)S(1)} %pad_maximum_fusion.2), channel_id=1, replica_groups=mesh['xh'=2,'y'=8,'core'=2,'xl'=2,'z'=8] {'xl','z'}, dimensions={0} | all-to-all | bytes 548864 | tf_op jit(solution)/shard_map/all_to_all | solution.py:118
  88.4 0.1 multiply_reduce_fusion.2
  88.6 14.2 %all_to_all.43.refs_1_ = bf16[16,64,128]{2,1,0:T(8,128)(2,1)S(1)} all-to-all(bf16[16,64,128]{2,1,0:T(8,128)(2,1)S(1)} %broadcast_in_dim.52), channel_id=1, replica_groups=mesh['xh'=2,'y'=8,'core'=2,'xl'=2,'z'=8] {'xl','z'}, dimensions={0} | all-to-all | bytes 524288 | tf_op jit(solution)/shard_map/all_to_all | solution.py:118
  102.8 1.4 shard_map.79
  104.2 0.1 multiply_convert_fusion.1
  104.2 2.2 %all-gather.2 = f16[32,64,128]{2,1,0:T(8,128)(2,1)S(1)} all-gather(f16[16,64,128]{2,1,0:T(8,128)(2,1)S(1)} %multiply_convert_fusion.1), channel_id=4, replica_groups=mesh['xh'=2,'y'=8,'core'=2,'xl'=2,'z'=8] {'core'}, dimensions={0}, use_global_device_ids=true | all-gather | bytes 786432 | tf_op jit(solution)/shard_map/all_gather | solution.py:127
  106.4 0.2 fusion.4
  106.6 16.3 %all_to_all.44 = f16[16,64,128]{2,1,0:T(8,128)(2,1)S(1)} all-to-all(f16[16,64,128]{2,1,0:T(8,128)(2,1)S(1)} %fusion.4), channel_id=1, replica_groups=mesh['xh'=2,'y'=8,'core'=2,'xl'=2,'z'=8] {'xh','y'}, dimensions={0} | all-to-all | bytes 524288 | tf_op jit(solution)/shard_map/all_to_all | solution.py:118
  122.9 0.1 multiply_reduce_fusion.1
  123.0 15.8 %all_to_all.45 = bf16[16,64,128]{2,1,0:T(8,128)(2,1)S(1)} all-to-all(bf16[16,64,128]{2,1,0:T(8,128)(2,1)S(1)} %broadcast_in_dim.53), channel_id=1, replica_groups=mesh['xh'=2,'y'=8,'core'=2,'xl'=2,'z'=8] {'xh','y'}, dimensions={0} | all-to-all | bytes 524288 | tf_op jit(solution)/shard_map/all_to_all | solution.py:118
  138.8 2.2 %all-gather.3 = bf16[32,64,128]{2,1,0:T(8,128)(2,1)S(1)} all-gather(bf16[16,64,128]{2,1,0:T(8,128)(2,1)S(1)} %all_to_all.45), channel_id=5, replica_groups=mesh['xh'=2,'y'=8,'core'=2,'xl'=2,'z'=8] {'core'}, dimensions={0}, use_global_device_ids=true | all-gather | bytes 786432 | tf_op jit(solution)/shard_map/all_gather | solution.py:189
  141.0 1.9 %shard_map.80 = (f32[16,64,128]{2,1,0:T(8,128)S(1)}, f32[64,128]{1,0:T(8,128)}) custom-call(s32[18]{0:T(128)S(1)} %pad_add_fusion.refs_0_, bf16[2,16,64,128]{3,2,1,0:T(8,128)(2,1)S(1)} %bitcast.12, bf16[8,512,512]{2,1,0:T(8,128)(2,1)S(1)} %copy-done.1, f32[64,128]{1,0:T(8,128)S(1)} %get-tuple-element.21.refs_3_), custom_call_target="tpu_custom_call" | custom-call | flops 268435456 | bytes 1048576 | tf_op jit(solution)/shard_map/pallas_call | solution.py:90
  142.9 0.1 multiply_convert_fusion
  143.0 14.6 %all_to_all.46 = f16[16,64,128]{2,1,0:T(8,128)(2,1)S(1)} all-to-all(f16[16,64,128]{2,1,0:T(8,128)(2,1)S(1)} %multiply_convert_fusion), channel_id=1, replica_groups=mesh['xh'=2,'y'=8,'core'=2,'xl'=2,'z'=8] {'xl','z'}, dimensions={0} | all-to-all | bytes 524288 | tf_op jit(solution)/shard_map/all_to_all | solution.py:118
  157.6 0.1 multiply_reduce_fusion
  157.6 0.6 multiply_add_fusion
  (22 shorter events, 0.4 us)
Async XLA Ops:
  2.2 21.5 %all-to-all-start = ((bf16[16,64,128]{2,1,0:T(8,128)(2,1)}), bf16[16,64,128]{2,1,0:T(8,128)(2,1)S(1)}, u32[]{:S(2)}, u32[]{:S(2)}) async-start(bf16[16,64,128]{2,1,0:T(8,128)(2,1)} %select_convert_fusion), calls=%async_computation | async-start | bytes 524288 | tf_op jit(solution)/shard_map/all_to_all | solution.py:118
  23.7 2.2 %copy-start = (bf16[8,512,512]{2,1,0:T(8,128)(2,1)S(1)}, bf16[8,512,512]{2,1,0:T(8,128)(2,1)}, u32[]{:S(2)}) copy-start(bf16[8,512,512]{2,1,0:T(8,128)(2,1)} %refs_2_.7) | copy-start | bytes 12582916
  27.6 43.3 %copy-start.1 = (bf16[8,512,512]{2,1,0:T(8,128)(2,1)S(1)}, bf16[8,512,512]{2,1,0:T(8,128)(2,1)}, u32[]{:S(2)}) copy-start(bf16[8,512,512]{2,1,0:T(8,128)(2,1)} %refs_2_.7) | copy-start | bytes 12582916
